TPU v7x, 512 devices: a whole 4x4x16 slice. The times are simulated.
512 devices in a mesh: atm: 32 (over z_lo, x, core), ocn: 16 (over y, z_hi).
Axes of the slice: x: 4, y: 4, z: 16 (z_hi: 4, z_lo: 4; z = z_hi * 4 + z_lo), core: 2. Of those that a mesh axis runs over, the one named last changes fastest.
Arguments:
- sky_velocity_tensor: bfloat16 [32, 32, 128, 512], P('ocn', 'atm'), may hold values from -6 to 6
- marine_tensor: bfloat16 [32, 64, 256, 256], P(None, 'ocn', 'atm'), may hold values from -6 to 6
- above_rotation_quarters: int32 [32], P('atm'), may hold values from 0 to 3
- beneath_rotation_quarters: int32 [32], P('atm'), may hold values from 0 to 3
- covering_pixels: int32 [64, 256, 4], P('ocn', 'atm'), may hold values from 0 to 7
- marine_pixel_indicator: int32 [64, 256], P('ocn', 'atm'), may hold values 0 or 1
- sky_stencil_filter: float32 [9, 512], replicated, may hold values from -2 to 2
- sky_scale_factor: float32 [512], replicated, may hold values from 0.1 to 1.9
- marine_heat_matrix: float32 [8, 512], replicated, may hold values from -2 to 2
- sky_expansion_matrix: bfloat16 [512, 1024], replicated, may hold values from -0.25 to 0.25
- sky_projection_matrix: bfloat16 [1024, 512], replicated, may hold values from -0.1875 to 0.1875
- exchange_output_matrix: bfloat16 [512, 16], replicated, may hold values from -0.25 to 0.25
- marine_stencil_filter: float32 [9, 256], replicated, may hold values from -2 to 2
- marine_scale_factor: float32 [256], replicated, may hold values from 0.1 to 1.9
- exchange_into_marine_matrix: float32 [16, 256], replicated, may hold values from -1.5 to 1.5
- marine_expansion_matrix: bfloat16 [256, 512], replicated, may hold values from -0.375 to 0.375
- marine_projection_matrix: bfloat16 [512, 256], replicated, may hold values from -0.25 to 0.25
- marine_interface_matrix: bfloat16 [256, 8], replicated, may hold values from -0.375 to 0.375
Outputs:
- air_out: bfloat16 [32, 32, 128, 512], P('ocn', 'atm')
- ocean_out: bfloat16 [32, 64, 256, 256], P(None, 'ocn', 'atm')
Inputs may be any that keep to these rules, and one draw needn't show every extreme that they name: `covering_pixels`: entries are indices m = row * 4 + column into the 2 x 4 atmosphere block under the ocean tile.
All inputs are finite; a program needn't handle non-finite values. No bound on the sum of `marine_pixel_indicator` on one device may be relied on, other than what follows from the above.
Results may differ from a plain program's by a relative error of at most 0.015.
Values may be sent and summed in bfloat16 or wider, within the bound.
A program may use at most 64 MiB of HBM per device.

v0:
```python
import jax
import jax.numpy as jnp
from jax import lax
from jax.sharding import PartitionSpec as P

NF = 16
K = 4
NSTEP = 2


def with_halo(cells, sides, width):
    for axis, dim in sides:
        count = lax.axis_size(axis)
        head = lax.slice_in_dim(cells, 0, width, axis=dim)
        tail = lax.slice_in_dim(cells, cells.shape[dim] - width, cells.shape[dim], axis=dim)
        cells = jnp.concatenate(
            [
                lax.ppermute(tail, axis, [(i, (i + 1) % count) for i in range(count)]),
                cells,
                lax.ppermute(head, axis, [((i + 1) % count, i) for i in range(count)]),
            ],
            axis=dim,
        )
    return cells


def rotate(values, code):
    half = values.shape[-1] // 2
    first = values[..., :half]
    second = values[..., half:]
    cosine = (code == 0).astype(jnp.float32) - (code == 2).astype(jnp.float32)
    sine = (code == 1).astype(jnp.float32) - (code == 3).astype(jnp.float32)
    return jnp.concatenate(
        [cosine * first - sine * second, sine * first + cosine * second], axis=-1
    )


def normalize(values, scale_factor):
    centre = jnp.mean(values, axis=-1, keepdims=True)
    shifted_vals = values - centre
    spread = jnp.mean(shifted_vals * shifted_vals, axis=-1, keepdims=True)
    return shifted_vals * lax.rsqrt(spread + 1e-05) * scale_factor


def pooled(values):
    shape = values.shape
    grouped = values.reshape(shape[0], shape[1] // 2, 2, shape[2] // 2, 2, shape[3])
    return jnp.sum(grouped, axis=(2, 4))


def sky_delta(
    sky_quantity,
    band_line_entries,
    pooled_marine_heat,
    stencil_filter,
    scale_factor,
    marine_heat_matrix,
    expansion_matrix,
    projection_matrix,
):
    accumulated_sum = jnp.einsum(
        "lved,dp->lvep", pooled_marine_heat, marine_heat_matrix, precision=lax.Precision.HIGHEST
    )
    for row_off in range(3):
        for col_off in range(3):
            accumulated_sum = accumulated_sum + stencil_filter[3 * row_off + col_off] * jnp.roll(
                band_line_entries[row_off], 1 - col_off, axis=2
            )
    width = sky_quantity.shape[-1]
    normed = normalize(accumulated_sum, scale_factor).astype(jnp.bfloat16).reshape(-1, width)
    hidden = jax.nn.gelu(
        jnp.dot(normed, expansion_matrix, preferred_element_type=jnp.float32), approximate=True
    ).astype(jnp.bfloat16)
    update = jnp.dot(hidden, projection_matrix, preferred_element_type=jnp.float32).reshape(
        sky_quantity.shape
    )
    return (sky_quantity.astype(jnp.float32) + update).astype(jnp.bfloat16)


def sea_update(
    marine_quantity,
    shifted,
    forcing_in,
    marine_indicator_real,
    stencil_filter,
    scale_factor,
    exchange_into_marine_matrix,
    expansion_matrix,
    projection_matrix,
):
    accumulated_sum = jnp.einsum(
        "brcf,fk->brck", forcing_in, exchange_into_marine_matrix, precision=lax.Precision.HIGHEST
    )
    for row_off in range(3):
        for col_off in range(3):
            accumulated_sum = accumulated_sum + stencil_filter[3 * row_off + col_off] * shifted(
                row_off, col_off
            )
    width = marine_quantity.shape[-1]
    normed = normalize(accumulated_sum, scale_factor).astype(jnp.bfloat16).reshape(-1, width)
    hidden = jax.nn.gelu(
        jnp.dot(normed, expansion_matrix, preferred_element_type=jnp.float32), approximate=True
    ).astype(jnp.bfloat16)
    update = jnp.dot(hidden, projection_matrix, preferred_element_type=jnp.float32).reshape(
        marine_quantity.shape
    )
    return (
        marine_quantity.astype(jnp.float32) + marine_indicator_real[None, :, :, None] * update
    ).astype(jnp.bfloat16)


def collect_interface_quantities(marine_quantity, marine_indicator_real, marine_interface_matrix):
    shape = marine_quantity.shape
    fine = jnp.dot(
        marine_quantity.reshape(-1, shape[3]),
        marine_interface_matrix,
        preferred_element_type=jnp.float32,
    )
    fine = fine.astype(jnp.bfloat16).reshape(shape[0], shape[1], shape[2], -1)
    masked = fine.astype(jnp.float32) * marine_indicator_real[None, :, :, None]
    flags = jnp.broadcast_to(
        marine_indicator_real[None, :, :, None], (shape[0], shape[1], shape[2], 1)
    ).astype(jnp.bfloat16)
    arrived, arrived_flags = (
        lax.all_to_all(
            lax.all_to_all(
                masked.astype(jnp.bfloat16), "ocn", split_axis=0, concat_axis=1, tiled=True
            ),
            "atm",
            split_axis=1,
            concat_axis=2,
            tiled=True,
        ),
        lax.all_to_all(
            lax.all_to_all(flags, "ocn", split_axis=0, concat_axis=1, tiled=True),
            "atm",
            split_axis=1,
            concat_axis=2,
            tiled=True,
        ),
    )
    sea_count = pooled(arrived_flags.astype(jnp.float32))
    return pooled(arrived.astype(jnp.float32)) / jnp.maximum(sea_count, 1.0)


def local(
    sky_velocity_tensor,
    marine_tensor,
    above_rotation_quarters,
    beneath_rotation_quarters,
    covering_pixels,
    marine_pixel_indicator,
    sky_stencil_filter,
    sky_scale_factor,
    marine_heat_matrix,
    sky_expansion_matrix,
    sky_projection_matrix,
    exchange_output_matrix,
    marine_stencil_filter,
    marine_scale_factor,
    exchange_into_marine_matrix,
    marine_expansion_matrix,
    marine_projection_matrix,
    marine_interface_matrix,
):
    samples, row_count, air_cols, channels = sky_velocity_tensor.shape
    batch, sea_rows, sea_cols, sea_chan = marine_tensor.shape
    marine_indicator_real = marine_pixel_indicator.astype(jnp.float32)
    block_cells = sea_rows // 2 * (sea_cols // 2)
    cell_ids = jnp.arange(block_cells, dtype=jnp.int32)
    spread_table = (
        jnp.sum((covering_pixels[..., None] == cell_ids).astype(jnp.float32), axis=2).reshape(
            sea_rows * sea_cols, block_cells
        )
        / K
    )
    codes_upper = above_rotation_quarters[None, :, None, None]
    codes_lower = beneath_rotation_quarters[None, :, None, None]
    sky_quantity = sky_velocity_tensor
    marine_quantity = marine_tensor
    for step in range(NSTEP):
        pooled_marine_heat = collect_interface_quantities(
            marine_quantity, marine_indicator_real, marine_interface_matrix
        )
        padded = with_halo(sky_quantity, (("atm", 1),), 1)
        above_adjacent = rotate(padded[:, :-2].astype(jnp.float32), codes_upper)
        centre_adjacent = padded[:, 1:-1].astype(jnp.float32)
        beneath_adjacent = rotate(padded[:, 2:].astype(jnp.float32), codes_lower)
        sky_quantity = sky_delta(
            sky_quantity,
            (above_adjacent, centre_adjacent, beneath_adjacent),
            pooled_marine_heat,
            sky_stencil_filter,
            sky_scale_factor,
            marine_heat_matrix,
            sky_expansion_matrix,
            sky_projection_matrix,
        )
        flux = jnp.dot(
            sky_quantity.reshape(-1, channels),
            exchange_output_matrix,
            preferred_element_type=jnp.float32,
        ).astype(jnp.bfloat16)
        flux = flux.reshape(samples, row_count, air_cols, NF)
        arrived = lax.all_to_all(
            lax.all_to_all(flux, "atm", split_axis=2, concat_axis=1, tiled=True),
            "ocn",
            split_axis=1,
            concat_axis=0,
            tiled=True,
        )
        flat = arrived.reshape(batch, block_cells, NF).astype(jnp.float32)
        forcing_in = jnp.einsum("nj,bjf->bnf", spread_table, flat, precision=lax.Precision.HIGHEST)
        forcing_in = forcing_in.reshape(batch, sea_rows, sea_cols, NF)
        framed = with_halo(marine_quantity, (("atm", 2), ("ocn", 1)), 1)

        def shifted(row_off, col_off, framed=framed):
            return framed[:, row_off : row_off + sea_rows, col_off : col_off + sea_cols].astype(
                jnp.float32
            )

        marine_quantity = sea_update(
            marine_quantity,
            shifted,
            forcing_in,
            marine_indicator_real,
            marine_stencil_filter,
            marine_scale_factor,
            exchange_into_marine_matrix,
            marine_expansion_matrix,
            marine_projection_matrix,
        )
    return (sky_quantity, marine_quantity)


def solution(mesh):
    return jax.shard_map(
        local,
        mesh=mesh,
        in_specs=(
            P("ocn", "atm", None, None),
            P(None, "ocn", "atm", None),
            P("atm"),
            P("atm"),
            P("ocn", "atm", None),
            P("ocn", "atm"),
            P(),
            P(),
            P(),
            P(),
            P(),
            P(),
            P(),
            P(),
            P(),
            P(),
            P(),
            P(),
        ),
        out_specs=(P("ocn", "atm", None, None), P(None, "ocn", "atm", None)),
        check_vma=False,
    )
```

profile of v0, /device:TPU:1, one launch (start us, length us, event | category | flops | bytes accessed | tf_op | source)
XLA Modules:
  0.0 287.6 jit_solution(13430261069601912783)
XLA Ops:
  0.6 4.6 %collective-permute-start = (bf16[2,1,128,512]{3,2,0,1:T(8,128)(2,1)}, bf16[2,1,128,512]{3,2,0,1:T(8,128)(2,1)S(1)}, u32[]{:S(2)}, u32[]{:S(2)}) collective-permute-start(bf16[2,1,128,512]{3,2,0,1:T(8,128)(2,1)} %bitcast.239), channel_id=1, source_target_pairs={{0,16},{16,32},{32,48},{48,64},{64,80},{80,96},{96,112},{112,128},... | collective-permute-start | bytes 786440 | tf_op jit(solution)/shard_map/ppermute | solution.py:18
  5.3 6.2 %collective-permute-start.1 = (bf16[2,1,128,512]{3,2,0,1:T(8,128)(2,1)}, bf16[2,1,128,512]{3,2,0,1:T(8,128)(2,1)}, u32[]{:S(2)}, u32[]{:S(2)}) collective-permute-start(bf16[2,1,128,512]{3,2,0,1:T(8,128)(2,1)} %bitcast.240), channel_id=1, source_target_pairs={{16,0},{32,16},{48,32},{64,48},{80,64},{96,80},{112,96},{128,112},... | collective-permute-start | bytes 786440 | tf_op jit(solution)/shard_map/ppermute | solution.py:20
  12.8 13.3 %all-to-all-start.2 = ((bf16[32,4,8,1]{2,1,3,0:T(4,128)(2,1)}), bf16[32,4,8,1]{2,1,3,0:T(4,128)(2,1)S(1)}, u32[]{:S(2)}, u32[]{:S(2)}) async-start(bf16[32,4,8,1]{2,1,3,0:T(4,128)(2,1)} %broadcast_in_dim.2), calls=%async_computation.2 | async-start | bytes 65536 | tf_op jit(solution)/shard_map/all_to_all | solution.py:135
  26.1 2.1 fusion.145
  28.2 3.9 %collective-permute-start.2 = (bf16[32,4,1,256]{3,2,1,0:T(2,128)(2,1)}, bf16[32,4,1,256]{3,2,1,0:T(2,128)(2,1)S(1)}, u32[]{:S(2)}, u32[]{:S(2)}) collective-permute-start(bf16[32,4,1,256]{3,2,1,0:T(2,128)(2,1)} %get-tuple-element.30), channel_id=1, source_target_pairs={{0,16},{16,32},{32,48},{48,64},{64,80},{80,96},{96,112},{112,128},... | collective-permute-start | bytes 196616 | tf_op jit(solution)/shard_map/ppermute | solution.py:18
  32.2 4.9 %collective-permute-start.3 = (bf16[32,4,1,256]{3,2,1,0:T(2,128)(2,1)}, bf16[32,4,1,256]{3,2,1,0:T(2,128)(2,1)S(1)}, u32[]{:S(2)}, u32[]{:S(2)}) collective-permute-start(bf16[32,4,1,256]{3,2,1,0:T(2,128)(2,1)} %get-tuple-element.31), channel_id=1, source_target_pairs={{16,0},{32,16},{48,32},{64,48},{80,64},{96,80},{112,96},{128,112},... | collective-permute-start | bytes 196616 | tf_op jit(solution)/shard_map/ppermute | solution.py:20
  42.5 9.1 %all-to-all-start.3 = ((bf16[2,64,8,1]{2,0,3,1:T(2,128)(2,1)}), bf16[2,64,8,1]{2,0,3,1:T(2,128)(2,1)S(1)}, u32[]{:S(2)}, u32[]{:S(2)}) async-start(bf16[2,64,8,1]{2,0,3,1:T(2,128)(2,1)} %copy.308), calls=%async_computation.3 | async-start | bytes 65536 | tf_op jit(solution)/shard_map/all_to_all | solution.py:134
  54.0 5.4 %all-to-all-done.3 = bf16[2,64,8,1]{2,0,3,1:T(2,128)(2,1)S(1)} async-done(((bf16[2,64,8,1]{2,0,3,1:T(2,128)(2,1)}), bf16[2,64,8,1]{2,0,3,1:T(2,128)(2,1)S(1)}, u32[]{:S(2)}, u32[]{:S(2)}) %all-to-all-start.3) | async-done | bytes 2080 | tf_op jit(solution)/shard_map/all_to_all | solution.py:134
  59.4 14.1 %all-to-all-start = ((bf16[16,2,256]{2,1,0:T(2,128)(2,1)}), bf16[16,2,256]{2,1,0:T(2,128)(2,1)S(1)}, u32[]{:S(2)}, u32[]{:S(2)}) async-start(bf16[16,2,256]{2,1,0:T(2,128)(2,1)} %reshape.562), calls=%async_computation | async-start | bytes 32768 | tf_op jit(solution)/shard_map/all_to_all | solution.py:126
  74.6 12.6 %all-to-all-done = bf16[16,2,256]{2,1,0:T(2,128)(2,1)S(1)} async-done(((bf16[16,2,256]{2,1,0:T(2,128)(2,1)}), bf16[16,2,256]{2,1,0:T(2,128)(2,1)S(1)}, u32[]{:S(2)}, u32[]{:S(2)}) %all-to-all-start) | async-done | bytes 16416 | tf_op jit(solution)/shard_map/all_to_all | solution.py:126
  88.6 5.3 %all-to-all-start.1 = ((bf16[32,2,128]{2,1,0:T(2,128)(2,1)}), bf16[32,2,128]{2,1,0:T(2,128)(2,1)S(1)}, u32[]{:S(2)}, u32[]{:S(2)}) async-start(bf16[32,2,128]{2,1,0:T(2,128)(2,1)} %reshape.564), calls=%async_computation.1 | async-start | bytes 32768 | tf_op jit(solution)/shard_map/all_to_all | solution.py:125
  93.9 1.1 pad_maximum_fusion.13
  95.0 2.2 collective-permute-start.4
  97.2 9.1 %collective-permute-start.5 = (bf16[32,1,10,256]{3,2,1,0:T(8,128)(2,1)}, bf16[32,1,10,256]{3,2,1,0:T(8,128)(2,1)}, u32[]{:S(2)}, u32[]{:S(2)}) collective-permute-start(bf16[32,1,10,256]{3,2,1,0:T(8,128)(2,1)} %get-tuple-element.27), channel_id=1, source_target_pairs={{1,0},{2,1},{3,2},{4,3},{5,4},{6,5},{7,6},{8,7},{9,8},{10,9},{11,1... | collective-permute-start | bytes 491528 | tf_op jit(solution)/shard_map/ppermute | solution.py:20
  110.1 1.3 fusion.151
  111.8 2.1 fusion.86
  115.6 8.4 %all-to-all-start.4 = ((bf16[2,1,128,16]{3,0,1,2:T(2,128)(2,1)}), bf16[2,1,128,16]{3,0,1,2:T(2,128)(2,1)S(1)}, u32[]{:S(2)}, u32[]{:S(2)}) async-start(bf16[2,1,128,16]{3,0,1,2:T(2,128)(2,1)} %copy.322), calls=%async_computation.4 | async-start | bytes 131072 | tf_op jit(solution)/shard_map/all_to_all | solution.py:206
  124.0 3.5 %collective-permute-done.4 = bf16[32,1,10,256]{3,2,1,0:T(8,128)(2,1)} collective-permute-done((bf16[32,1,10,256]{3,2,1,0:T(8,128)(2,1)}, bf16[32,1,10,256]{3,2,1,0:T(8,128)(2,1)}, u32[]{:S(2)}, u32[]{:S(2)}) %collective-permute-start.4) | collective-permute-done | bytes 163872 | tf_op jit(solution)/shard_map/ppermute | solution.py:18
  127.5 3.8 %maximum_maximum_fusion = (bf16[32,5,10,256]{3,2,1,0:T(8,128)(2,1)}, bf16[32,5,10,256]{3,2,1,0:T(8,128)(2,1)}) fusion(bf16[32,4,1,256]{3,2,1,0:T(2,128)(2,1)S(1)} %collective-permute-done.3, bf16[32,4,8,256]{3,2,1,0:T(8,128)(2,1)S(1)} %copy-done.1, bf16[32,4,1,256]{3,2,1,0:T(2,128)(2,1)S(1)} %collective-permute-done.2, ...), kind=kLoop, calls=%fused_computation.26 | loop fusion | flops 6553600 | bytes 2621440 | tf_op jit(solution)/shard_map/concatenate | solution.py:16
  131.2 4.9 %collective-permute-start.6 = (bf16[2,1,128,512]{3,2,0,1:T(8,128)(2,1)S(1)}, bf16[2,1,128,512]{3,2,0,1:T(8,128)(2,1)S(1)}, u32[]{:S(2)}, u32[]{:S(2)}) collective-permute-start(bf16[2,1,128,512]{3,2,0,1:T(8,128)(2,1)S(1)} %get-tuple-element.19), channel_id=1, source_target_pairs={{0,16},{16,32},{32,48},{48,64},{64,80},{80,96},{96,112},{112,128},... | collective-permute-start | bytes 786440 | tf_op jit(solution)/shard_map/ppermute | solution.py:18
  136.1 1.9 collective-permute-start.7
  138.8 9.4 %all-to-all-start.5 = ((bf16[16,2,128]{2,1,0:T(2,128)(2,1)}), bf16[16,2,128]{2,1,0:T(2,128)(2,1)S(1)}, u32[]{:S(2)}, u32[]{:S(2)}) async-start(bf16[16,2,128]{2,1,0:T(2,128)(2,1)} %reshape.566), calls=%async_computation.5 | async-start | bytes 16384 | tf_op jit(solution)/shard_map/all_to_all | solution.py:205
  149.2 12.6 %all-to-all-done.5 = bf16[16,2,128]{2,1,0:T(2,128)(2,1)S(1)} async-done(((bf16[16,2,128]{2,1,0:T(2,128)(2,1)}), bf16[16,2,128]{2,1,0:T(2,128)(2,1)S(1)}, u32[]{:S(2)}, u32[]{:S(2)}) %all-to-all-start.5) | async-done | bytes 8224 | tf_op jit(solution)/shard_map/all_to_all | solution.py:205
  162.4 1.0 copy.361
  163.5 5.5 %fusion.152 = (f32[32,4,8]{2,1,0:T(4,128)S(1)}, f32[32,4,8,256]{3,2,1,0:T(8,128)S(1)}) fusion(bf16[32,5,10,256]{3,2,1,0:T(8,128)(2,1)} %get-tuple-element.25, f32[256]{0:T(256)S(1)} %bitcast.303, f32[256]{0:T(256)S(1)} %bitcast.305, f32[256]{0:T(256)S(1)} %bitcast.291, bf16[32,4,1,256]{3,2,1,0:T(2,128)(2,1)S(1)} %collective-permute-done.3, ...), kind=kOutput, calls=%fused_computation.264 | convolution fusion | flops 59243520 | bytes 4944896 | tf_op jit(solution)/shard_map/brcf,fk->brck/dot_general | solution.py:91
  169.7 1.1 multiply_convert_fusion.1
  170.8 2.9 %fusion.17 = f32[1024,256]{1,0:T(8,128)} fusion(bf16[512,256]{1,0:T(8,128)(2,1)S(1)} %copy-done.63, bf16[1024,256]{1,0:T(8,128)(2,1)} %bitcast.251, bf16[256,512]{1,0:T(8,128)(2,1)S(1)} %copy-done.65), kind=kOutput, calls=%fused_computation.21 | convolution fusion | flops 541589504 | bytes 2097152 | tf_op jit(solution)/shard_map/dot_general | solution.py:104
  173.8 1.5 fusion.43
  176.1 5.1 %collective-permute-start.8 = (bf16[32,4,1,256]{3,2,1,0:T(2,128)(2,1)}, bf16[32,4,1,256]{3,2,1,0:T(2,128)(2,1)S(1)}, u32[]{:S(2)}, u32[]{:S(2)}) collective-permute-start(bf16[32,4,1,256]{3,2,1,0:T(2,128)(2,1)} %get-tuple-element.28), channel_id=1, source_target_pairs={{0,16},{16,32},{32,48},{48,64},{64,80},{80,96},{96,112},{112,128},... | collective-permute-start | bytes 196616 | tf_op jit(solution)/shard_map/ppermute | solution.py:18
  181.2 2.9 collective-permute-start.9
  186.6 3.4 %all-to-all-start.6 = ((bf16[16,2,256]{2,1,0:T(2,128)(2,1)}), bf16[16,2,256]{2,1,0:T(2,128)(2,1)S(1)}, u32[]{:S(2)}, u32[]{:S(2)}) async-start(bf16[16,2,256]{2,1,0:T(2,128)(2,1)} %reshape.568), calls=%async_computation.6 | async-start | bytes 32768 | tf_op jit(solution)/shard_map/all_to_all | solution.py:126
  191.3 12.2 %all-to-all-done.6 = bf16[16,2,256]{2,1,0:T(2,128)(2,1)S(1)} async-done(((bf16[16,2,256]{2,1,0:T(2,128)(2,1)}), bf16[16,2,256]{2,1,0:T(2,128)(2,1)S(1)}, u32[]{:S(2)}, u32[]{:S(2)}) %all-to-all-start.6) | async-done | bytes 16416 | tf_op jit(solution)/shard_map/all_to_all | solution.py:126
  204.9 10.4 %all-to-all-start.7 = ((bf16[32,2,128]{2,1,0:T(2,128)(2,1)}), bf16[32,2,128]{2,1,0:T(2,128)(2,1)S(1)}, u32[]{:S(2)}, u32[]{:S(2)}) async-start(bf16[32,2,128]{2,1,0:T(2,128)(2,1)} %reshape.570), calls=%async_computation.7 | async-start | bytes 32768 | tf_op jit(solution)/shard_map/all_to_all | solution.py:125
  215.3 1.9 pad_maximum_fusion.10
  217.2 2.2 collective-permute-start.10
  219.4 9.3 %collective-permute-start.11 = (bf16[32,1,10,256]{3,2,1,0:T(8,128)(2,1)}, bf16[32,1,10,256]{3,2,1,0:T(8,128)(2,1)}, u32[]{:S(2)}, u32[]{:S(2)}) collective-permute-start(bf16[32,1,10,256]{3,2,1,0:T(8,128)(2,1)} %get-tuple-element.23), channel_id=1, source_target_pairs={{1,0},{2,1},{3,2},{4,3},{5,4},{6,5},{7,6},{8,7},{9,8},{10,9},{11,1... | collective-permute-start | bytes 491528 | tf_op jit(solution)/shard_map/ppermute | solution.py:20
  229.1 1.0 reduce_sum.146
  231.2 1.1 slice_maximum_fusion
  234.7 1.3 fusion.153
  236.4 2.1 fusion.84
  238.9 17.5 %all_to_all.145 = bf16[2,1,128,16]{3,0,1,2:T(2,128)(2,1)S(1)} all-to-all(bf16[2,1,128,16]{3,0,1,2:T(2,128)(2,1)S(1)} %copy.342), channel_id=1, replica_groups=mesh['atm'=32,'ocn'=16] {'atm'}, dimensions={2} | all-to-all | bytes 16384 | tf_op jit(solution)/shard_map/all_to_all | solution.py:206
  257.1 5.7 %all-to-all-start.9 = ((bf16[16,2,128]{2,1,0:T(2,128)(2,1)}), bf16[16,2,128]{2,1,0:T(2,128)(2,1)S(1)}, u32[]{:S(2)}, u32[]{:S(2)}) async-start(bf16[16,2,128]{2,1,0:T(2,128)(2,1)} %reshape.572), calls=%async_computation.9 | async-start | bytes 16384 | tf_op jit(solution)/shard_map/all_to_all | solution.py:205
  262.9 3.8 %maximum_maximum_fusion.1 = (bf16[32,5,10,256]{3,2,1,0:T(8,128)(2,1)}, bf16[32,5,10,256]{3,2,1,0:T(8,128)(2,1)}) fusion(bf16[32,4,1,256]{3,2,1,0:T(2,128)(2,1)} %collective-permute-done.9, bf16[32,4,8,256]{3,2,1,0:T(8,128)(2,1)S(1)} %fusion.43, bf16[32,4,1,256]{3,2,1,0:T(2,128)(2,1)S(1)} %collective-permute-done.8, ...), kind=kLoop, calls=%fused_computation.28 | loop fusion | flops 6553600 | bytes 2621440 | tf_op jit(solution)/shard_map/concatenate | solution.py:16
  266.8 9.6 %all-to-all-done.9 = bf16[16,2,128]{2,1,0:T(2,128)(2,1)S(1)} async-done(((bf16[16,2,128]{2,1,0:T(2,128)(2,1)}), bf16[16,2,128]{2,1,0:T(2,128)(2,1)S(1)}, u32[]{:S(2)}, u32[]{:S(2)}) %all-to-all-start.9) | async-done | bytes 8224 | tf_op jit(solution)/shard_map/all_to_all | solution.py:205
  277.3 5.3 %fusion.154 = (f32[32,4,8]{2,1,0:T(4,128)S(1)}, f32[32,4,8,256]{3,2,1,0:T(8,128)S(1)}) fusion(bf16[32,5,10,256]{3,2,1,0:T(8,128)(2,1)} %get-tuple-element.21, f32[256]{0:T(256)S(1)} %bitcast.304, f32[256]{0:T(256)S(1)} %bitcast.306, f32[256]{0:T(256)S(1)} %bitcast.292, bf16[32,4,1,256]{3,2,1,0:T(2,128)(2,1)} %collective-permute-done.9, ...), kind=kOutput, calls=%fused_computation.266 | convolution fusion | flops 59243520 | bytes 4944896 | tf_op jit(solution)/shard_map/brcf,fk->brck/dot_general | solution.py:91
  283.4 1.2 multiply_convert_fusion
  284.5 2.0 fusion.16
  286.6 1.0 fusion.49
  (259 shorter events, 31.0 us)
Async XLA Ops:
  0.6 111.1 %copy-start = (bf16[1024,512]{1,0:T(8,128)(2,1)S(1)}, bf16[1024,512]{1,0:T(8,128)(2,1)}, u32[]{:S(2)}) copy-start(bf16[1024,512]{1,0:T(8,128)(2,1)} %param.28) | copy-start | bytes 3145732
  0.6 106.4 %collective-permute-start = (bf16[2,1,128,512]{3,2,0,1:T(8,128)(2,1)}, bf16[2,1,128,512]{3,2,0,1:T(8,128)(2,1)S(1)}, u32[]{:S(2)}, u32[]{:S(2)}) collective-permute-start(bf16[2,1,128,512]{3,2,0,1:T(8,128)(2,1)} %bitcast.239), channel_id=1, source_target_pairs={{0,16},{16,32},{32,48},{48,64},{64,80},{80,96},{96,112},{112,128},... | collective-permute-start | bytes 786440 | tf_op jit(solution)/shard_map/ppermute | solution.py:18
  5.3 102.5 %collective-permute-start.1 = (bf16[2,1,128,512]{3,2,0,1:T(8,128)(2,1)}, bf16[2,1,128,512]{3,2,0,1:T(8,128)(2,1)}, u32[]{:S(2)}, u32[]{:S(2)}) collective-permute-start(bf16[2,1,128,512]{3,2,0,1:T(8,128)(2,1)} %bitcast.240), channel_id=1, source_target_pairs={{16,0},{32,16},{48,32},{64,48},{80,64},{96,80},{112,96},{128,112},... | collective-permute-start | bytes 786440 | tf_op jit(solution)/shard_map/ppermute | solution.py:20
  12.2 28.9 %copy-start.9 = (f32[4,8]{1,0:T(4,128)}, f32[4,8]{1,0:T(4,128)S(1)}, u32[]{:S(2)}) copy-start(f32[4,8]{1,0:T(4,128)S(1)} %get-tuple-element.81) | copy-start | bytes 388
  12.8 29.0 %all-to-all-start.2 = ((bf16[32,4,8,1]{2,1,3,0:T(4,128)(2,1)}), bf16[32,4,8,1]{2,1,3,0:T(4,128)(2,1)S(1)}, u32[]{:S(2)}, u32[]{:S(2)}) async-start(bf16[32,4,8,1]{2,1,3,0:T(4,128)(2,1)} %broadcast_in_dim.2), calls=%async_computation.2 | async-start | bytes 65536 | tf_op jit(solution)/shard_map/all_to_all | solution.py:135
  28.2 65.6 %collective-permute-start.2 = (bf16[32,4,1,256]{3,2,1,0:T(2,128)(2,1)}, bf16[32,4,1,256]{3,2,1,0:T(2,128)(2,1)S(1)}, u32[]{:S(2)}, u32[]{:S(2)}) collective-permute-start(bf16[32,4,1,256]{3,2,1,0:T(2,128)(2,1)} %get-tuple-element.30), channel_id=1, source_target_pairs={{0,16},{16,32},{32,48},{48,64},{64,80},{80,96},{96,112},{112,128},... | collective-permute-start | bytes 196616 | tf_op jit(solution)/shard_map/ppermute | solution.py:18
  32.2 8.0 %copy-start.1 = (bf16[32,4,8,256]{3,2,1,0:T(8,128)(2,1)S(1)}, bf16[32,4,8,256]{3,2,1,0:T(8,128)(2,1)}, u32[]{:S(2)}) copy-start(bf16[32,4,8,256]{3,2,1,0:T(8,128)(2,1)} %param.19) | copy-start | bytes 1572868
  32.2 8.0 %copy-start.12 = (bf16[256,8]{0,1:T(8,128)(2,1)S(1)}, bf16[256,8]{0,1:T(8,128)(2,1)}, u32[]{:S(2)}) copy-start(bf16[256,8]{0,1:T(8,128)(2,1)} %param.35) | copy-start | bytes 12292
  32.2 61.7 %collective-permute-start.3 = (bf16[32,4,1,256]{3,2,1,0:T(2,128)(2,1)}, bf16[32,4,1,256]{3,2,1,0:T(2,128)(2,1)S(1)}, u32[]{:S(2)}, u32[]{:S(2)}) collective-permute-start(bf16[32,4,1,256]{3,2,1,0:T(2,128)(2,1)} %get-tuple-element.31), channel_id=1, source_target_pairs={{16,0},{32,16},{48,32},{64,48},{80,64},{96,80},{112,96},{128,112},... | collective-permute-start | bytes 196616 | tf_op jit(solution)/shard_map/ppermute | solution.py:20
  38.9 12.7 %copy-start.17 = (s32[4,8,4]{1,2,0:T(4,128)S(1)}, s32[4,8,4]{1,2,0:T(4,128)}, u32[]{:S(2)}) copy-start(s32[4,8,4]{1,2,0:T(4,128)} %param.22) | copy-start | bytes 1540
  42.5 16.9 %all-to-all-start.3 = ((bf16[2,64,8,1]{2,0,3,1:T(2,128)(2,1)}), bf16[2,64,8,1]{2,0,3,1:T(2,128)(2,1)S(1)}, u32[]{:S(2)}, u32[]{:S(2)}) async-start(bf16[2,64,8,1]{2,0,3,1:T(2,128)(2,1)} %copy.308), calls=%async_computation.3 | async-start | bytes 65536 | tf_op jit(solution)/shard_map/all_to_all | solution.py:134
  59.4 27.8 %all-to-all-start = ((bf16[16,2,256]{2,1,0:T(2,128)(2,1)}), bf16[16,2,256]{2,1,0:T(2,128)(2,1)S(1)}, u32[]{:S(2)}, u32[]{:S(2)}) async-start(bf16[16,2,256]{2,1,0:T(2,128)(2,1)} %reshape.562), calls=%async_computation | async-start | bytes 32768 | tf_op jit(solution)/shard_map/all_to_all | solution.py:126
  88.6 17.7 %all-to-all-start.1 = ((bf16[32,2,128]{2,1,0:T(2,128)(2,1)}), bf16[32,2,128]{2,1,0:T(2,128)(2,1)S(1)}, u32[]{:S(2)}, u32[]{:S(2)}) async-start(bf16[32,2,128]{2,1,0:T(2,128)(2,1)} %reshape.564), calls=%async_computation.1 | async-start | bytes 32768 | tf_op jit(solution)/shard_map/all_to_all | solution.py:125
  95.0 32.5 %collective-permute-start.4 = (bf16[32,1,10,256]{3,2,1,0:T(8,128)(2,1)}, bf16[32,1,10,256]{3,2,1,0:T(8,128)(2,1)}, u32[]{:S(2)}, u32[]{:S(2)}) collective-permute-start(bf16[32,1,10,256]{3,2,1,0:T(8,128)(2,1)} %get-tuple-element.26), channel_id=1, source_target_pairs={{0,1},{1,2},{2,3},{3,4},{4,5},{5,6},{6,7},{7,8},{8,9},{9,10},{10,1... | collective-permute-start | bytes 491528 | tf_op jit(solution)/shard_map/ppermute | solution.py:18
  97.2 30.3 %collective-permute-start.5 = (bf16[32,1,10,256]{3,2,1,0:T(8,128)(2,1)}, bf16[32,1,10,256]{3,2,1,0:T(8,128)(2,1)}, u32[]{:S(2)}, u32[]{:S(2)}) collective-permute-start(bf16[32,1,10,256]{3,2,1,0:T(8,128)(2,1)} %get-tuple-element.27), channel_id=1, source_target_pairs={{1,0},{2,1},{3,2},{4,3},{5,4},{6,5},{7,6},{8,7},{9,8},{10,9},{11,1... | collective-permute-start | bytes 491528 | tf_op jit(solution)/shard_map/ppermute | solution.py:20
  115.6 22.5 %all-to-all-start.4 = ((bf16[2,1,128,16]{3,0,1,2:T(2,128)(2,1)}), bf16[2,1,128,16]{3,0,1,2:T(2,128)(2,1)S(1)}, u32[]{:S(2)}, u32[]{:S(2)}) async-start(bf16[2,1,128,16]{3,0,1,2:T(2,128)(2,1)} %copy.322), calls=%async_computation.4 | async-start | bytes 131072 | tf_op jit(solution)/shard_map/all_to_all | solution.py:206
  131.2 98.9 %collective-permute-start.6 = (bf16[2,1,128,512]{3,2,0,1:T(8,128)(2,1)S(1)}, bf16[2,1,128,512]{3,2,0,1:T(8,128)(2,1)S(1)}, u32[]{:S(2)}, u32[]{:S(2)}) collective-permute-start(bf16[2,1,128,512]{3,2,0,1:T(8,128)(2,1)S(1)} %get-tuple-element.19), channel_id=1, source_target_pairs={{0,16},{16,32},{32,48},{48,64},{64,80},{80,96},{96,112},{112,128},... | collective-permute-start | bytes 786440 | tf_op jit(solution)/shard_map/ppermute | solution.py:18
  136.1 96.2 %collective-permute-start.7 = (bf16[2,1,128,512]{3,2,0,1:T(8,128)(2,1)S(1)}, bf16[2,1,128,512]{3,2,0,1:T(8,128)(2,1)}, u32[]{:S(2)}, u32[]{:S(2)}) collective-permute-start(bf16[2,1,128,512]{3,2,0,1:T(8,128)(2,1)S(1)} %get-tuple-element.19), channel_id=1, source_target_pairs={{16,0},{32,16},{48,32},{64,48},{80,64},{96,80},{112,96},{128,112},... | collective-permute-start | bytes 786440 | tf_op jit(solution)/shard_map/ppermute | solution.py:20
  138.8 23.0 %all-to-all-start.5 = ((bf16[16,2,128]{2,1,0:T(2,128)(2,1)}), bf16[16,2,128]{2,1,0:T(2,128)(2,1)S(1)}, u32[]{:S(2)}, u32[]{:S(2)}) async-start(bf16[16,2,128]{2,1,0:T(2,128)(2,1)} %reshape.566), calls=%async_computation.5 | async-start | bytes 16384 | tf_op jit(solution)/shard_map/all_to_all | solution.py:205
  148.2 15.2 %copy-start.43 = (f32[1,256]{1,0:T(1,128)S(1)}, f32[1,256]{1,0:T(1,128)}, u32[]{:S(2)}) copy-start(f32[1,256]{1,0:T(1,128)} %get-tuple-element.71) | copy-start | bytes 3076
  148.2 15.2 %copy-start.45 = (f32[1,256]{1,0:T(1,128)S(1)}, f32[1,256]{1,0:T(1,128)}, u32[]{:S(2)}) copy-start(f32[1,256]{1,0:T(1,128)} %get-tuple-element.72) | copy-start | bytes 3076
  148.3 15.2 %copy-start.47 = (f32[1,256]{1,0:T(1,128)S(1)}, f32[1,256]{1,0:T(1,128)}, u32[]{:S(2)}) copy-start(f32[1,256]{1,0:T(1,128)} %get-tuple-element.73) | copy-start | bytes 3076
  148.3 15.2 %copy-start.49 = (f32[1,256]{1,0:T(1,128)S(1)}, f32[1,256]{1,0:T(1,128)}, u32[]{:S(2)}) copy-start(f32[1,256]{1,0:T(1,128)} %get-tuple-element.74) | copy-start | bytes 3076
  148.3 15.2 %copy-start.51 = (f32[1,256]{1,0:T(1,128)S(1)}, f32[1,256]{1,0:T(1,128)}, u32[]{:S(2)}) copy-start(f32[1,256]{1,0:T(1,128)} %get-tuple-element.75) | copy-start | bytes 3076
  148.3 15.2 %copy-start.53 = (f32[1,256]{1,0:T(1,128)S(1)}, f32[1,256]{1,0:T(1,128)}, u32[]{:S(2)}) copy-start(f32[1,256]{1,0:T(1,128)} %get-tuple-element.76) | copy-start | bytes 3076
  148.3 15.2 %copy-start.55 = (f32[1,256]{1,0:T(1,128)S(1)}, f32[1,256]{1,0:T(1,128)}, u32[]{:S(2)}) copy-start(f32[1,256]{1,0:T(1,128)} %get-tuple-element.77) | copy-start | bytes 3076
  148.3 15.2 %copy-start.57 = (f32[1,256]{1,0:T(1,128)S(1)}, f32[1,256]{1,0:T(1,128)}, u32[]{:S(2)}) copy-start(f32[1,256]{1,0:T(1,128)} %get-tuple-element.78) | copy-start | bytes 3076
  148.3 15.2 %copy-start.59 = (f32[1,256]{1,0:T(1,128)S(1)}, f32[1,256]{1,0:T(1,128)}, u32[]{:S(2)}) copy-start(f32[1,256]{1,0:T(1,128)} %get-tuple-element.79) | copy-start | bytes 3076
  148.3 15.2 %copy-start.68 = (f32[16,256]{1,0:T(8,128)S(1)}, f32[16,256]{1,0:T(8,128)}, u32[]{:S(2)}) copy-start(f32[16,256]{1,0:T(8,128)} %param.32) | copy-start | bytes 49156
  173.8 10.3 %copy-start.13 = (bf16[256,8]{0,1:T(8,128)(2,1)S(1)}, bf16[256,8]{0,1:T(8,128)(2,1)}, u32[]{:S(2)}) copy-start(bf16[256,8]{0,1:T(8,128)(2,1)} %param.35) | copy-start | bytes 12292
  176.1 39.1 %collective-permute-start.8 = (bf16[32,4,1,256]{3,2,1,0:T(2,128)(2,1)}, bf16[32,4,1,256]{3,2,1,0:T(2,128)(2,1)S(1)}, u32[]{:S(2)}, u32[]{:S(2)}) collective-permute-start(bf16[32,4,1,256]{3,2,1,0:T(2,128)(2,1)} %get-tuple-element.28), channel_id=1, source_target_pairs={{0,16},{16,32},{32,48},{48,64},{64,80},{80,96},{96,112},{112,128},... | collective-permute-start | bytes 196616 | tf_op jit(solution)/shard_map/ppermute | solution.py:18
  181.2 34.0 %collective-permute-start.9 = (bf16[32,4,1,256]{3,2,1,0:T(2,128)(2,1)}, bf16[32,4,1,256]{3,2,1,0:T(2,128)(2,1)}, u32[]{:S(2)}, u32[]{:S(2)}) collective-permute-start(bf16[32,4,1,256]{3,2,1,0:T(2,128)(2,1)} %get-tuple-element.29), channel_id=1, source_target_pairs={{16,0},{32,16},{48,32},{64,48},{80,64},{96,80},{112,96},{128,112},... | collective-permute-start | bytes 196616 | tf_op jit(solution)/shard_map/ppermute | solution.py:20
  186.6 16.9 %all-to-all-start.6 = ((bf16[16,2,256]{2,1,0:T(2,128)(2,1)}), bf16[16,2,256]{2,1,0:T(2,128)(2,1)S(1)}, u32[]{:S(2)}, u32[]{:S(2)}) async-start(bf16[16,2,256]{2,1,0:T(2,128)(2,1)} %reshape.568), calls=%async_computation.6 | async-start | bytes 32768 | tf_op jit(solution)/shard_map/all_to_all | solution.py:126
  204.9 23.8 %all-to-all-start.7 = ((bf16[32,2,128]{2,1,0:T(2,128)(2,1)}), bf16[32,2,128]{2,1,0:T(2,128)(2,1)S(1)}, u32[]{:S(2)}, u32[]{:S(2)}) async-start(bf16[32,2,128]{2,1,0:T(2,128)(2,1)} %reshape.570), calls=%async_computation.7 | async-start | bytes 32768 | tf_op jit(solution)/shard_map/all_to_all | solution.py:125
  217.2 45.7 %collective-permute-start.10 = (bf16[32,1,10,256]{3,2,1,0:T(8,128)(2,1)}, bf16[32,1,10,256]{3,2,1,0:T(8,128)(2,1)}, u32[]{:S(2)}, u32[]{:S(2)}) collective-permute-start(bf16[32,1,10,256]{3,2,1,0:T(8,128)(2,1)} %get-tuple-element.22), channel_id=1, source_target_pairs={{0,1},{1,2},{2,3},{3,4},{4,5},{5,6},{6,7},{7,8},{8,9},{9,10},{10,1... | collective-permute-start | bytes 491528 | tf_op jit(solution)/shard_map/ppermute | solution.py:18
  219.4 43.5 %collective-permute-start.11 = (bf16[32,1,10,256]{3,2,1,0:T(8,128)(2,1)}, bf16[32,1,10,256]{3,2,1,0:T(8,128)(2,1)}, u32[]{:S(2)}, u32[]{:S(2)}) collective-permute-start(bf16[32,1,10,256]{3,2,1,0:T(8,128)(2,1)} %get-tuple-element.23), channel_id=1, source_target_pairs={{1,0},{2,1},{3,2},{4,3},{5,4},{6,5},{7,6},{8,7},{9,8},{10,9},{11,1... | collective-permute-start | bytes 491528 | tf_op jit(solution)/shard_map/ppermute | solution.py:20
  238.5 28.1 %copy-start.3 = (bf16[2,1,128,512]{3,2,0,1:T(8,128)(2,1)}, bf16[2,1,128,512]{3,2,0,1:T(8,128)(2,1)S(1)}, u32[]{:S(2)}) copy-start(bf16[2,1,128,512]{3,2,0,1:T(8,128)(2,1)S(1)} %add_convert_fusion) | copy-start | bytes 786436
  257.1 19.2 %all-to-all-start.9 = ((bf16[16,2,128]{2,1,0:T(2,128)(2,1)}), bf16[16,2,128]{2,1,0:T(2,128)(2,1)S(1)}, u32[]{:S(2)}, u32[]{:S(2)}) async-start(bf16[16,2,128]{2,1,0:T(2,128)(2,1)} %reshape.572), calls=%async_computation.9 | async-start | bytes 16384 | tf_op jit(solution)/shard_map/all_to_all | solution.py:205
  266.7 10.6 %copy-start.44 = (f32[1,256]{1,0:T(1,128)S(1)}, f32[1,256]{1,0:T(1,128)}, u32[]{:S(2)}) copy-start(f32[1,256]{1,0:T(1,128)} %get-tuple-element.71) | copy-start | bytes 3076
  266.7 10.6 %copy-start.46 = (f32[1,256]{1,0:T(1,128)S(1)}, f32[1,256]{1,0:T(1,128)}, u32[]{:S(2)}) copy-start(f32[1,256]{1,0:T(1,128)} %get-tuple-element.72) | copy-start | bytes 3076
  266.7 10.6 %copy-start.48 = (f32[1,256]{1,0:T(1,128)S(1)}, f32[1,256]{1,0:T(1,128)}, u32[]{:S(2)}) copy-start(f32[1,256]{1,0:T(1,128)} %get-tuple-element.73) | copy-start | bytes 3076
  266.7 10.6 %copy-start.50 = (f32[1,256]{1,0:T(1,128)S(1)}, f32[1,256]{1,0:T(1,128)}, u32[]{:S(2)}) copy-start(f32[1,256]{1,0:T(1,128)} %get-tuple-element.74) | copy-start | bytes 3076
  266.7 10.6 %copy-start.52 = (f32[1,256]{1,0:T(1,128)S(1)}, f32[1,256]{1,0:T(1,128)}, u32[]{:S(2)}) copy-start(f32[1,256]{1,0:T(1,128)} %get-tuple-element.75) | copy-start | bytes 3076
  266.7 10.6 %copy-start.54 = (f32[1,256]{1,0:T(1,128)S(1)}, f32[1,256]{1,0:T(1,128)}, u32[]{:S(2)}) copy-start(f32[1,256]{1,0:T(1,128)} %get-tuple-element.76) | copy-start | bytes 3076
  266.7 10.6 %copy-start.56 = (f32[1,256]{1,0:T(1,128)S(1)}, f32[1,256]{1,0:T(1,128)}, u32[]{:S(2)}) copy-start(f32[1,256]{1,0:T(1,128)} %get-tuple-element.77) | copy-start | bytes 3076
  266.7 10.6 %copy-start.58 = (f32[1,256]{1,0:T(1,128)S(1)}, f32[1,256]{1,0:T(1,128)}, u32[]{:S(2)}) copy-start(f32[1,256]{1,0:T(1,128)} %get-tuple-element.78) | copy-start | bytes 3076
  266.7 10.6 %copy-start.60 = (f32[1,256]{1,0:T(1,128)S(1)}, f32[1,256]{1,0:T(1,128)}, u32[]{:S(2)}) copy-start(f32[1,256]{1,0:T(1,128)} %get-tuple-element.79) | copy-start | bytes 3076
  266.8 10.6 %copy-start.69 = (f32[16,256]{1,0:T(8,128)S(1)}, f32[16,256]{1,0:T(8,128)}, u32[]{:S(2)}) copy-start(f32[16,256]{1,0:T(8,128)} %param.32) | copy-start | bytes 49156
  (43 other events, 59.0 us)
where the time goes:
time: 289 us; the launch traced here: 288 us
  starting transfers between devices  136 us (47%)
  waiting for transfers between devices  55.9 us (19%)
  other arithmetic  26.8 us (9%)
  matrix products  24 us (8%)
  local copies, waits for them, and re-layouts  23.4 us (8%)
  blocking collectives  17.5 us (6%)
  between operations  3.74 us (1%)
    ppermute x6, starting transfers between devices, with_halo(): lax.ppermute(head, axis, [((i + 1) % count, i) for i in range(count)])  34.2 us
    all_to_all x2, waiting for transfers between devices, collect_interface_quantities(): lax.all_to_all(masked.astype(jnp.bfloat16), 'ocn', split_axis=0, concat_a...  24.7 us
    ppermute x6, starting transfers between devices, with_halo(): lax.ppermute(tail, axis, [(i, (i + 1) % count) for i in range(count)])  22.9 us
    all_to_all x2, waiting for transfers between devices, local(): lax.all_to_all(lax.all_to_all(flux, 'atm', split_axis=2, concat_axis=1, t...  22.2 us
    all_to_all x2, starting transfers between devices, collect_interface_quantities(): lax.all_to_all(masked.astype(jnp.bfloat16), 'ocn', split_axis=0, concat_a...  17.6 us
    all_to_all x1, blocking collectives, local(): lax.all_to_all(flux, 'atm', split_axis=2, concat_axis=1, tiled=True)  17.5 us
    all_to_all x2, starting transfers between devices, collect_interface_quantities(): lax.all_to_all(lax.all_to_all(masked.astype(jnp.bfloat16), 'ocn', split_a...  15.6 us
    all_to_all x2, starting transfers between devices, local(): lax.all_to_all(lax.all_to_all(flux, 'atm', split_axis=2, concat_axis=1, t...  15.1 us
  transfers between devices with their start and end apart: 21, of which 6 were waited for; matrix products, arithmetic and copies ran while one was open for 21% of the time, Pallas kernels for 0%

commit v1 on v0

v1 whole, which is shorter than its diff:
```python
import functools

import jax
import jax.numpy as jnp
from jax import lax
from jax.experimental import pallas as pl
from jax.experimental.pallas import tpu as pltpu
from jax.sharding import PartitionSpec as P

MESH = pl.DeviceIdType.MESH
F32 = jnp.float32
BF16 = jnp.bfloat16
NSTEP = 2
SIDES = [(-1, 0), (1, 0), (0, -1), (0, 1), (-1, -1), (-1, 1), (1, -1), (1, 1)]


def gelu(x):
    inner = x * (0.7978845608028654 + 0.035677408136300125 * (x * x))
    half = 0.5 * x
    return half + half * jnp.tanh(inner)


def normed(z, gain):
    shifted = z - jnp.mean(z, axis=-1, keepdims=True)
    spread = jnp.mean(shifted * shifted, axis=-1, keepdims=True)
    return (shifted * lax.rsqrt(spread + 1e-05) * gain).astype(BF16)


def spread_over_lanes(rows, lanes):
    r = lax.broadcasted_iota(jnp.int32, (rows, lanes), 0)
    c = lax.broadcasted_iota(jnp.int32, (rows, lanes), 1)
    return (lax.rem(c, rows) == r).astype(BF16)


def kernel(
    na, no,
    above, beneath, cover, sea_flag,
    sky, sea, sky_filter, sky_gain, heat, sky_in, sky_back, to_flux, sea_filter, sea_gain, from_flux, sea_in, sea_back, to_sst,
    sky_out, sea_out,
    raw_sky, raw_sea, v_sky_filter, v_sky_gain, v_heat, v_sky_in, v_sky_back, v_to_flux, v_sea_filter, v_sea_gain, v_from_flux,
    v_sea_in, v_sea_back, v_to_sst,
    tok_sky, tok_sea, air, up, down, ocean, ext, zbuf, ubuf, hbuf,
    flux_wide, heat_wide, into_wide, sst_wide, cellw, seaw, poolw,
    sst_tx, sst_rx, flux_tx, flux_rx,
    in_sem, sst_send, sst_recv, flux_send, flux_recv, self_sem, air_send, air_recv, sea_send, sea_recv, out_sem,
):
    a = lax.axis_index("atm")
    o = lax.axis_index("ocn")
    half_a = a // 2
    mine = half_a == o

    def at(atm, ocn):
        return {"atm": lax.rem(atm + na, na), "ocn": lax.rem(ocn + no, no)}

    def is_me(atm, ocn):
        return jnp.logical_and(atm == a, ocn == o)

    barrier = pltpu.get_barrier_semaphore()

    def greet_a(k, c):
        for rr in range(2):
            @pl.when(jnp.logical_not(is_me(2 * o + rr, k)))
            def _():
                pl.semaphore_signal(barrier, inc=1, device_id=at(2 * o + rr, k), device_id_type=MESH)
        return c

    def greet_b(q, c):
        @pl.when(jnp.logical_not(is_me(q, half_a)))
        def _():
            pl.semaphore_signal(barrier, inc=1, device_id=at(q, half_a), device_id_type=MESH)
        return c

    lax.fori_loop(0, no, greet_a, 0)
    lax.fori_loop(0, na, greet_b, 0)
    for di, dj in SIDES:
        pl.semaphore_signal(barrier, inc=1, device_id=at(a + dj, o + di), device_id_type=MESH)

    loads = [
        pltpu.make_async_copy(src, dst, in_sem.at[n])
        for n, (src, dst) in enumerate([
            (sea, raw_sea), (sky, raw_sky), (to_sst, v_to_sst), (sky_filter, v_sky_filter), (heat, v_heat),
            (sky_gain, v_sky_gain), (sky_in, v_sky_in), (sky_back, v_sky_back), (to_flux, v_to_flux),
            (sea_filter, v_sea_filter), (sea_gain, v_sea_gain), (from_flux, v_from_flux), (sea_in, v_sea_in),
            (sea_back, v_sea_back),
        ])
    ]
    for load in loads:
        load.start()

    lane = lax.broadcasted_iota(jnp.int32, (no, 128), 1)

    def tables(cell, c):
        row, col = cell // 8, lax.rem(cell, 8)
        flag = jnp.full((no, 256), sea_flag[row, col], jnp.int32).astype(F32)
        r0, c0 = row // 2 * 2, col // 2 * 2
        count = sea_flag[r0, c0] + sea_flag[r0, c0 + 1] + sea_flag[r0 + 1, c0] + sea_flag[r0 + 1, c0 + 1]
        count = jnp.full((no, 256), count, jnp.int32).astype(F32)
        seaw[cell] = flag
        poolw[cell] = flag / jnp.maximum(count, 1.0)
        share = jnp.zeros((no, 128), F32)
        for k in range(4):
            share = share + jnp.where(lane // 16 == cover[row, k, col], 0.25, 0.0)
        cellw[cell] = share
        return c

    lax.fori_loop(0, 32, tables, 0)

    loads[0].wait()
    per = 2 * no // 4

    def open_sea(n, c):
        part = raw_sea[pl.ds(n * per, per)].astype(F32)
        part = part.reshape(per * 32, 256)
        for w in range(2):
            tok_sea[w, pl.ds(pl.multiple_of(n * per * 32, per * 32), per * 32), :] = part[:, 128 * w : 128 * w + 128]
        return c

    lax.fori_loop(0, 4, open_sea, 0)

    def sort_sea(cell, c):
        row, col = cell // 8, lax.rem(cell, 8)
        for par in range(2):
            for w in range(2):
                part = tok_sea[w, pl.ds(par * 32 + cell, no, stride=64), :]
                ocean[0, par, 1 + row, 1 + col, :, 128 * w : 128 * w + 128] = part.astype(BF16)
        return c

    lax.fori_loop(0, 32, sort_sea, 0)

    loads[1].wait()
    for w in range(4):
        tok_sky[w] = raw_sky[:, :, :, 128 * w : 128 * w + 128].astype(F32).reshape(8 * na, 128)

    def sort_sky(cc, c):
        for par in range(2):
            for w in range(4):
                part = tok_sky[w, pl.ds(par * 4 * na + cc, na, stride=4), :]
                air[0, par, cc, :, 128 * w : 128 * w + 128] = part.astype(BF16)
        return c

    lax.fori_loop(0, 4, sort_sky, 0)

    loads[2].wait()
    sst_wide[...] = lax.dot_general(
        v_to_sst[...], spread_over_lanes(8, 128), (((0,), (0,)), ((), ())), preferred_element_type=F32
    ).astype(BF16)

    def put_air(step, par):
        return [
            pltpu.make_async_remote_copy(
                src_ref=air.at[step, par], dst_ref=there.at[step, par], send_sem=air_send.at[step, par, n],
                recv_sem=air_recv.at[step, par, n], device_id=at(a + da, o), device_id_type=MESH,
            )
            for n, (there, da) in enumerate([(up, 1), (down, -1)])
        ]

    def put_sea(step, par):
        copies = []
        for n, (di, dj) in enumerate(SIDES):
            rows = {-1: 1, 0: pl.ds(1, 4), 1: 4}[di]
            cols = {-1: 1, 0: pl.ds(1, 8), 1: 8}[dj]
            to_rows = {-1: 5, 0: pl.ds(1, 4), 1: 0}[di]
            to_cols = {-1: 9, 0: pl.ds(1, 8), 1: 0}[dj]
            copies.append(
                pltpu.make_async_remote_copy(
                    src_ref=ocean.at[step, par, rows, cols], dst_ref=ocean.at[step, par, to_rows, to_cols],
                    send_sem=sea_send.at[step, par, n], recv_sem=sea_recv.at[step, par, n],
                    device_id=at(a + dj, o + di), device_id_type=MESH,
                )
            )
        return copies

    def start(copies):
        for copy in copies:
            copy.start()

    def send_sst(step, par):
        def block_rows(rr, c):
            parts = []
            for cc in range(4):
                sums = jnp.zeros((no, 256), F32)
                for i in range(2):
                    for j in range(2):
                        cell = (2 * rr + i) * 8 + 2 * cc + j
                        sums = sums + poolw[cell] * ocean[step, par, 1 + 2 * rr + i, 1 + 2 * cc + j].astype(F32)
                parts.append(sums.astype(BF16))
            lines = jnp.zeros((no, 128), F32)
            which = lax.rem(lane // 8, 4)
            for cc in range(4):
                got = jnp.dot(parts[cc], sst_wide[...], preferred_element_type=F32)
                lines = jnp.where(which == cc, got, lines)
            sst_tx[step, par, pl.ds(rr * no, no)] = lines.reshape(no, 1, 128)
            return c

        lax.fori_loop(0, 2, block_rows, 0)

        def put(k, c):
            for rr in range(2):
                src = sst_tx.at[step, par, rr * no + k]
                dst = sst_rx.at[step, par, a]
                there = is_me(2 * o + rr, k)

                @pl.when(jnp.logical_not(there))
                def _():
                    pltpu.make_async_remote_copy(
                        src_ref=src, dst_ref=dst, send_sem=sst_send.at[step, par], recv_sem=sst_recv.at[step, par],
                        device_id=at(2 * o + rr, k), device_id_type=MESH,
                    ).start()

                @pl.when(there)
                def _():
                    pltpu.make_async_copy(src, dst, self_sem.at[step, par, 0]).start()
            return c

        lax.fori_loop(0, no, put, 0)

    def send_flux(step, par):
        def put(q, c):
            src = flux_tx.at[step, par, q]
            dst = flux_rx.at[step, par, lax.rem(a, 2) * no + o]
            there = is_me(q, half_a)

            @pl.when(jnp.logical_not(there))
            def _():
                pltpu.make_async_remote_copy(
                    src_ref=src, dst_ref=dst, send_sem=flux_send.at[step, par], recv_sem=flux_recv.at[step, par],
                    device_id=at(q, half_a), device_id_type=MESH,
                ).start()

            @pl.when(there)
            def _():
                pltpu.make_async_copy(src, dst, self_sem.at[step, par, 1]).start()
            return c

        lax.fori_loop(0, na, put, 0)

    def rows_of(buf, sem_send, sem_recv, step, par, count):
        part = buf.at[step, par, pl.ds(0, count)]
        return pltpu.make_async_remote_copy(
            src_ref=part, dst_ref=part, send_sem=sem_send.at[step, par], recv_sem=sem_recv.at[step, par],
            device_id=at(a, o), device_id_type=MESH,
        )

    def exchange_wait(buf, sem_send, sem_recv, step, par, n, received):
        @pl.when(mine)
        def _():
            copy = rows_of(buf, sem_send, sem_recv, step, par, na - 1)
            if received:
                pltpu.make_async_copy(buf.at[step, par, 0], buf.at[step, par, 0], self_sem.at[step, par, n]).wait()
                copy.wait_recv()
            else:
                copy.wait_send()

        @pl.when(jnp.logical_not(mine))
        def _():
            copy = rows_of(buf, sem_send, sem_recv, step, par, na)
            if received:
                copy.wait_recv()
            else:
                copy.wait_send()


    @pl.when(mine)
    def _():
        pl.semaphore_wait(barrier, 2 * na + 6)

    @pl.when(jnp.logical_not(mine))
    def _():
        pl.semaphore_wait(barrier, 2 * na + 8)

    for par in range(2):
        start(put_air(0, par))
    for par in range(2):
        send_sst(0, par)
    for par in range(2):
        start(put_sea(0, par))

    for load in loads[3:]:
        load.wait()
    flux_wide[...] = lax.dot_general(
        v_to_flux[...], spread_over_lanes(16, 128), (((0,), (0,)), ((), ())), preferred_element_type=F32
    ).astype(BF16)
    heat_wide[...] = lax.dot_general(
        spread_over_lanes(8, 128), v_heat[...].astype(BF16), (((0,), (0,)), ((), ())), preferred_element_type=F32
    ).astype(BF16)
    into_wide[...] = lax.dot_general(
        spread_over_lanes(16, 128), v_from_flux[...].astype(BF16), (((0,), (0,)), ((), ())), preferred_element_type=F32
    ).astype(BF16)

    turns = []
    for code in (above[0], beneath[0]):
        cosine = jnp.where(code == 0, 1.0, 0.0) - jnp.where(code == 2, 1.0, 0.0)
        sine = jnp.where(code == 1, 1.0, 0.0) - jnp.where(code == 3, 1.0, 0.0)
        turns.append((cosine, sine))

    lane_a = lax.broadcasted_iota(jnp.int32, (na, 128), 1)

    def sky_part(step, par):
        for copy in put_air(step, par):
            copy.wait_recv()

        def frame(cc, c):
            ext[1, cc + 1] = air[step, par, cc].astype(F32)
            for n, src in ((0, up), (2, down)):
                cosine, sine = turns[n // 2]
                east = src[step, par, cc, :, :256].astype(F32)
                north = src[step, par, cc, :, 256:].astype(F32)
                ext[n, cc + 1, :, :256] = cosine * east - sine * north
                ext[n, cc + 1, :, 256:] = sine * east + cosine * north
            return c

        lax.fori_loop(0, 4, frame, 0)

        def ends(n, c):
            ext[n, 0] = pltpu.roll(ext[n, 4], 1, 0)
            ext[n, 5] = pltpu.roll(ext[n, 1], na - 1, 0)
            return c

        lax.fori_loop(0, 3, ends, 0)

        exchange_wait(sst_rx, sst_send, sst_recv, step, par, 0, True)
        fields = sst_rx[step, par].reshape(na, 128)
        for cc in range(4):
            one = jnp.where(lane_a // 8 == cc, fields, 0.0).astype(BF16)
            zbuf[cc] = jnp.dot(one, heat_wide[...], preferred_element_type=F32)

        def column(cc, c):
            z = zbuf[cc]
            for i in range(3):
                for j in range(3):
                    z = z + v_sky_filter[3 * i + j : 3 * i + j + 1, :] * ext[i, cc + j]
            ubuf[cc] = normed(z, v_sky_gain[...])
            return c

        lax.fori_loop(0, 4, column, 0)
        u = ubuf[...].reshape(4 * na, 512)
        for n in range(4):
            part = slice(256 * n, 256 * n + 256)
            hbuf[:, part] = gelu(jnp.dot(u, v_sky_in[:, part], preferred_element_type=F32)).astype(BF16)
        for n in range(2):
            part = slice(256 * n, 256 * n + 256)
            change = jnp.dot(hbuf[...], v_sky_back[:, part], preferred_element_type=F32)
            old = air[step, par, :, :, part].astype(F32)
            air[step + 1, par, :, :, part] = (old + change.reshape(4, na, 256)).astype(BF16)
        lines = jnp.zeros((na, 128), F32)
        for cc in range(4):
            got = jnp.dot(air[step + 1, par, cc], flux_wide[...], preferred_element_type=F32)
            lines = jnp.where(lax.rem(lane_a // 16, 4) == cc, got, lines)
        flux_tx[step, par] = lines.reshape(na, 1, 128)
        send_flux(step, par)

        @pl.when(step + 1 < NSTEP)
        def _():
            start(put_air(step + 1, par))

        @pl.when(step + 1 == NSTEP)
        def _():
            pltpu.make_async_copy(air.at[step + 1, par], sky_out.at[par], out_sem.at[par]).start()

    def sea_part(step, par):
        for copy in put_sea(step, par):
            copy.wait_recv()
        exchange_wait(flux_rx, flux_send, flux_recv, step, par, 1, True)
        got = flux_rx[step, par].reshape(2 * no, 128)
        fields = jnp.where(lane < 64, got[:no], got[no:])

        def line(row, c):
            cells = pl.ds(pl.multiple_of(row * 8, 8), 8)
            lhs = (cellw[cells] * fields[None]).astype(BF16).reshape(8 * no, 128)
            z = jnp.dot(lhs, into_wide[...], preferred_element_type=F32).reshape(8, no, 256)
            for i in range(3):
                for j in range(3):
                    tap = v_sea_filter[3 * i + j : 3 * i + j + 1, :]
                    z = z + tap[None] * ocean[step, par, row + i, j : j + 8].astype(F32)
            u = normed(z.reshape(8 * no, 256), v_sea_gain[...])
            hidden = gelu(jnp.dot(u, v_sea_in[...], preferred_element_type=F32)).astype(BF16)
            change = jnp.dot(hidden, v_sea_back[...], preferred_element_type=F32).reshape(8, no, 256)
            old = ocean[step, par, row + 1, 1:9].astype(F32)
            ocean[step + 1, par, row + 1, 1:9] = (old + seaw[cells] * change).astype(BF16)
            return c

        lax.fori_loop(0, 4, line, 0)

        @pl.when(step + 1 < NSTEP)
        def _():
            send_sst(step + 1, par)
            start(put_sea(step + 1, par))

        @pl.when(step + 1 == NSTEP)
        def _():
            pltpu.make_async_copy(
                ocean.at[step + 1, par, pl.ds(1, 4), pl.ds(1, 8)], sea_out.at[par], out_sem.at[2 + par]
            ).start()

    def one_step(step, c):
        def sky_loop(par, c):
            sky_part(step, par)
            return c

        def sea_loop(par, c):
            sea_part(step, par)
            return c

        lax.fori_loop(0, 2, sky_loop, 0)
        lax.fori_loop(0, 2, sea_loop, 0)
        return c

    lax.fori_loop(0, NSTEP, one_step, 0)

    def close(n, c):
        step, par = n // 2, lax.rem(n, 2)
        for copy in put_air(step, par) + put_sea(step, par):
            copy.wait_send()
        exchange_wait(sst_tx, sst_send, sst_recv, step, par, 0, False)
        exchange_wait(flux_tx, flux_send, flux_recv, step, par, 1, False)
        return c

    lax.fori_loop(0, 2 * NSTEP, close, 0)
    for par in range(2):
        pltpu.make_async_copy(air.at[NSTEP, par], sky_out.at[par], out_sem.at[par]).wait()
        pltpu.make_async_copy(
            ocean.at[NSTEP, par, pl.ds(1, 4), pl.ds(1, 8)], sea_out.at[par], out_sem.at[2 + par]
        ).wait()


def local(na, no, sky, sea, above, beneath, cover, sea_flag, sky_filter, sky_gain, heat, sky_in, sky_back, to_flux,
          sea_filter, sea_gain, from_flux, sea_in, sea_back, to_sst):
    smem = pl.BlockSpec(memory_space=pltpu.SMEM)
    hbm = pl.BlockSpec(memory_space=pl.ANY)
    vmem = pltpu.VMEM
    dma = pltpu.SemaphoreType.DMA
    n, p = NSTEP, 2
    big = [sky, sea, sky_filter, sky_gain[None], heat, sky_in, sky_back, to_flux.T, sea_filter, sea_gain[None], from_flux, sea_in,
           sea_back, to_sst.T]
    sky_new, sea_new = pl.pallas_call(
        functools.partial(kernel, na, no),
        out_shape=(
            jax.ShapeDtypeStruct((p, 4, na, 512), BF16),
            jax.ShapeDtypeStruct((p, 4, 8, no, 256), BF16),
        ),
        in_specs=[smem] * 4 + [hbm] * len(big),
        out_specs=(hbm, hbm),
        scratch_shapes=[vmem(x.shape, x.dtype) for x in big] + [
            vmem((4, p * 4 * na, 128), F32),
            vmem((2, 2 * no * 32, 128), F32),
            vmem((n + 1, p, 4, na, 512), BF16),
            vmem((n, p, 4, na, 512), BF16),
            vmem((n, p, 4, na, 512), BF16),
            vmem((n + 1, p, 6, 10, no, 256), BF16),
            vmem((3, 6, na, 512), F32),
            vmem((4, na, 512), F32),
            vmem((4, na, 512), BF16),
            vmem((4 * na, 1024), BF16),
            vmem((512, 128), BF16),
            vmem((128, 512), BF16),
            vmem((128, 256), BF16),
            vmem((256, 128), BF16),
            vmem((32, no, 128), F32),
            vmem((32, no, 256), F32),
            vmem((32, no, 256), F32),
            vmem((n, p, na, 1, 128), F32),
            vmem((n, p, na, 1, 128), F32),
            vmem((n, p, na, 1, 128), F32),
            vmem((n, p, na, 1, 128), F32),
            dma((len(big),)),
            dma((n, p)),
            dma((n, p)),
            dma((n, p)),
            dma((n, p)),
            dma((n, p, 2)),
            dma((n, p, 2)),
            dma((n, p, 2)),
            dma((n, p, 8)),
            dma((n, p, 8)),
            dma((4,)),
        ],
        compiler_params=pltpu.CompilerParams(
            collective_id=0, has_side_effects=True, vmem_limit_bytes=56 * 1024 * 1024
        ),
        name="coupled_steps",
    )(above, beneath, cover.transpose(0, 2, 1), sea_flag, *big)
    sky_new = sky_new.transpose(0, 2, 1, 3).reshape(sky.shape)
    sea_new = sea_new.transpose(3, 0, 1, 2, 4).reshape(sea.shape)
    return sky_new, sea_new


def solution(mesh):
    return jax.shard_map(
        functools.partial(local, mesh.shape["atm"], mesh.shape["ocn"]),
        mesh=mesh,
        in_specs=(
            P("ocn", "atm", None, None),
            P(None, "ocn", "atm", None),
            P("atm"),
            P("atm"),
            P("ocn", "atm", None),
            P("ocn", "atm"),
        ) + (P(),) * 12,
        out_specs=(P("ocn", "atm", None, None), P(None, "ocn", "atm", None)),
        check_vma=False,
    )
```

time: 289 us -> 96.3 us (0.33)
  starting transfers between devices: 136 us -> 0 us
  Pallas kernels: 0 us -> 90.3 us
  waiting for transfers between devices: 55.9 us -> 0 us
  other arithmetic: 26.8 us -> 0 us
  matrix products: 24 us -> 0 us
  local copies, waits for them, and re-layouts: 23.4 us -> 2.97 us
  blocking collectives: 17.5 us -> 0 us
    pallas_call x0 -> x1, Pallas kernels: none -> 90.3 us  [local(): pl.pallas_call(functools.partial(kernel, na, no), out_shape=(jax.ShapeDty...]
    all_to_all x9 -> x0, starting transfers between devices: 79.1 us -> none  [the longest x2 17.6 us: collect_interface_quantities(): lax.all_to_all(masked.astype(jnp.bfloat16), 'ocn', split_axis=0, concat_a...]
    ppermute x12 -> x0, starting transfers between devices: 57.1 us -> none  [the longest x6 34.2 us: with_halo(): lax.ppermute(head, axis, [((i + 1) % count, i) for i in range(count)])]
    all_to_all x9 -> x0, waiting for transfers between devices: 52.4 us -> none  [the longest x2 24.7 us: collect_interface_quantities(): lax.all_to_all(masked.astype(jnp.bfloat16), 'ocn', split_axis=0, concat_a...]
    dot_general x14 -> x0, matrix products: 24 us -> none  [the longest x2 10.8 us: sea_update(): jnp.einsum('brcf,fk->brck', forcing_in, exchange_into_marine_matrix, prec...]
    all_to_all x1 -> x0, blocking collectives: 17.5 us -> none  [local(): lax.all_to_all(flux, 'atm', split_axis=2, concat_axis=1, tiled=True)]
    convert_element_type x14 -> x0, other arithmetic: 9.03 us -> none  [the longest x2 2.49 us: sea_update(): return (marine_quantity.astype(jnp.float32) + marine_indicator_real[None,...]
    concatenate x10 -> x0, other arithmetic: 9.03 us -> none  [the longest x2 7.57 us: with_halo(): jnp.concatenate([lax.ppermute(tail, axis, [(i, (i + 1) % count) for i in...]
  transfers between devices with their start and end apart: 21 -> 0, of which waited for: 6 -> 0; matrix products, arithmetic and copies ran while one was open for 21% -> 0% of each run, Pallas kernels for 0% -> 0%
where the time goes in v1:
time: 96.3 us; the launch traced here: 95.2 us
  Pallas kernels  90.3 us (94%)
  local copies, waits for them, and re-layouts  2.97 us (3%)
  between operations  1.95 us (2%)
    pallas_call x1, Pallas kernels, local(): pl.pallas_call(functools.partial(kernel, na, no), out_shape=(jax.ShapeDty...  90.3 us

profile of v1, /device:TPU:1, one launch (start us, length us, event | category | flops | bytes accessed | tf_op | source)
XLA Modules:
  0.0 95.2 jit_solution(2892137708329156031)
XLA Ops:
  1.9 90.3 %coupled_steps.1 = (bf16[2,4,32,512]{3,2,1,0:T(8,128)(2,1)}, bf16[2,4,8,16,256]{4,3,2,1,0:T(8,128)(2,1)}) custom-call(s32[1]{0:T(128)S(6)} %copy.23.above, s32[1]{0:T(128)S(6)} %copy.24.beneath, s32[4,4,8]{2,1,0:T(4,128)} %bitcast.14, s32[4,8]{1,0:T(4,128)} %sea_flag.1, bf16[2,1,128,512]{3,2,1,0:T(8,128)(2,1)} %sky.1, bf16[32,4,8,256]{3,2,1,0:T(8,128)(2,1)} %sea.1, ...), custom_call_target="tpu_custom_call" | custom-call | tf_op jit(solution)/shard_map/coupled_steps/pallas_call | solution.py:435
  92.3 0.0 copy-start
  92.3 1.3 %copy.20 = bf16[2,32,4,512]{3,0,2,1:T(2,128)(2,1)S(1)} copy(bf16[2,32,4,512]{3,1,2,0:T(8,128)(2,1)} %bitcast.12) | data formatting | bytes 524288 | tf_op jit(solution)/shard_map/transpose | solution.py:482
  93.6 0.7 copy.22
  94.3 0.0 copy-done
  94.3 1.0 %copy.21 = bf16[16,2,4,8,256]{4,3,2,1,0:T(8,128)(2,1)} copy(bf16[16,2,4,8,256]{4,0,3,2,1:T(8,128)(2,1)S(1)} %bitcast.11) | data formatting | bytes 1048576 | tf_op jit(solution)/shard_map/transpose | solution.py:483
Async XLA Ops:
  92.3 2.0 %copy-start = (bf16[2,4,8,16,256]{4,3,2,1,0:T(8,128)(2,1)S(1)}, bf16[2,4,8,16,256]{4,3,2,1,0:T(8,128)(2,1)}, u32[]{:S(2)}) copy-start(bf16[2,4,8,16,256]{4,3,2,1,0:T(8,128)(2,1)} %get-tuple-element.5) | copy-start | bytes 1572868

commit v2 on v1

--- a/solution.py
+++ b/solution.py
@@ -55,26 +55,6 @@
     def is_me(atm, ocn):
         return jnp.logical_and(atm == a, ocn == o)
 
-    barrier = pltpu.get_barrier_semaphore()
-
-    def greet_a(k, c):
-        for rr in range(2):
-            @pl.when(jnp.logical_not(is_me(2 * o + rr, k)))
-            def _():
-                pl.semaphore_signal(barrier, inc=1, device_id=at(2 * o + rr, k), device_id_type=MESH)
-        return c
-
-    def greet_b(q, c):
-        @pl.when(jnp.logical_not(is_me(q, half_a)))
-        def _():
-            pl.semaphore_signal(barrier, inc=1, device_id=at(q, half_a), device_id_type=MESH)
-        return c
-
-    lax.fori_loop(0, no, greet_a, 0)
-    lax.fori_loop(0, na, greet_b, 0)
-    for di, dj in SIDES:
-        pl.semaphore_signal(barrier, inc=1, device_id=at(a + dj, o + di), device_id_type=MESH)
-
     loads = [
         pltpu.make_async_copy(src, dst, in_sem.at[n])
         for n, (src, dst) in enumerate([
@@ -87,9 +67,24 @@
     for load in loads:
         load.start()
 
+    barrier = pltpu.get_barrier_semaphore()
+
+    def greet(n, c):
+        pl.semaphore_signal(barrier, inc=1, device_id=at(a + n, half_a), device_id_type=MESH)
+        return c
+
+    lax.fori_loop(1, na, greet, 0)
+
+    @pl.when(jnp.logical_not(mine))
+    def _():
+        pl.semaphore_signal(barrier, inc=1, device_id=at(a, half_a), device_id_type=MESH)
+
+    for di, dj in SIDES:
+        pl.semaphore_signal(barrier, inc=1, device_id=at(a + dj, o + di), device_id_type=MESH)
+
     lane = lax.broadcasted_iota(jnp.int32, (no, 128), 1)
 
-    def tables(cell, c):
+    def pool_table(cell, c):
         row, col = cell // 8, lax.rem(cell, 8)
         flag = jnp.full((no, 256), sea_flag[row, col], jnp.int32).astype(F32)
         r0, c0 = row // 2 * 2, col // 2 * 2
@@ -97,13 +92,17 @@
         count = jnp.full((no, 256), count, jnp.int32).astype(F32)
         seaw[cell] = flag
         poolw[cell] = flag / jnp.maximum(count, 1.0)
+        return c
+
+    lax.fori_loop(0, 32, pool_table, 0)
+
+    def cell_table(cell, c):
+        row, col = cell // 8, lax.rem(cell, 8)
         share = jnp.zeros((no, 128), F32)
         for k in range(4):
             share = share + jnp.where(lane // 16 == cover[row, k, col], 0.25, 0.0)
         cellw[cell] = share
         return c
-
-    lax.fori_loop(0, 32, tables, 0)
 
     loads[0].wait()
     per = 2 * no // 4
@@ -117,28 +116,15 @@
 
     lax.fori_loop(0, 4, open_sea, 0)
 
-    def sort_sea(cell, c):
-        row, col = cell // 8, lax.rem(cell, 8)
-        for par in range(2):
+    def sort_sea(par):
+        def sort_cell(cell, c):
+            row, col = cell // 8, lax.rem(cell, 8)
             for w in range(2):
                 part = tok_sea[w, pl.ds(par * 32 + cell, no, stride=64), :]
                 ocean[0, par, 1 + row, 1 + col, :, 128 * w : 128 * w + 128] = part.astype(BF16)
-        return c
-
-    lax.fori_loop(0, 32, sort_sea, 0)
-
-    loads[1].wait()
-    for w in range(4):
-        tok_sky[w] = raw_sky[:, :, :, 128 * w : 128 * w + 128].astype(F32).reshape(8 * na, 128)
-
-    def sort_sky(cc, c):
-        for par in range(2):
-            for w in range(4):
-                part = tok_sky[w, pl.ds(par * 4 * na + cc, na, stride=4), :]
-                air[0, par, cc, :, 128 * w : 128 * w + 128] = part.astype(BF16)
-        return c
-
-    lax.fori_loop(0, 4, sort_sky, 0)
+            return c
+
+        lax.fori_loop(0, 32, sort_cell, 0)
 
     loads[2].wait()
     sst_wide[...] = lax.dot_general(
@@ -174,7 +160,7 @@
         for copy in copies:
             copy.start()
 
-    def send_sst(step, par):
+    def make_sst(step, par):
         def block_rows(rr, c):
             parts = []
             for cc in range(4):
@@ -194,45 +180,65 @@
 
         lax.fori_loop(0, 2, block_rows, 0)
 
-        def put(k, c):
-            for rr in range(2):
-                src = sst_tx.at[step, par, rr * no + k]
-                dst = sst_rx.at[step, par, a]
-                there = is_me(2 * o + rr, k)
-
-                @pl.when(jnp.logical_not(there))
-                def _():
-                    pltpu.make_async_remote_copy(
-                        src_ref=src, dst_ref=dst, send_sem=sst_send.at[step, par], recv_sem=sst_recv.at[step, par],
-                        device_id=at(2 * o + rr, k), device_id_type=MESH,
-                    ).start()
-
-                @pl.when(there)
-                def _():
-                    pltpu.make_async_copy(src, dst, self_sem.at[step, par, 0]).start()
-            return c
-
-        lax.fori_loop(0, no, put, 0)
+    def send_sst(step, par):
+        def put(ocn, rr):
+            return pltpu.make_async_remote_copy(
+                src_ref=sst_tx.at[step, par, rr * no + ocn], dst_ref=sst_rx.at[step, par, a],
+                send_sem=sst_send.at[step, par], recv_sem=sst_recv.at[step, par],
+                device_id=at(2 * o + rr, ocn), device_id_type=MESH,
+            )
+
+        apart = min(4, no)
+        for d in sorted(range(apart), key=lambda d: -min(d, apart - d)):
+            def put_group(y, c, d=d):
+                ocn = y * apart + lax.rem(o + d, apart)
+                if d:
+                    for rr in range(2):
+                        put(ocn, rr).start()
+                else:
+                    for rr in range(2):
+                        @pl.when(jnp.logical_not(is_me(2 * o + rr, ocn)))
+                        def _():
+                            put(ocn, rr).start()
+                return c
+
+            lax.fori_loop(0, no // apart, put_group, 0)
+
+        @pl.when(mine)
+        def _():
+            pltpu.make_async_copy(
+                sst_tx.at[step, par, lax.rem(a, 2) * no + o], sst_rx.at[step, par, a], self_sem.at[step, par, 0]
+            ).start()
 
     def send_flux(step, par):
-        def put(q, c):
-            src = flux_tx.at[step, par, q]
-            dst = flux_rx.at[step, par, lax.rem(a, 2) * no + o]
-            there = is_me(q, half_a)
-
-            @pl.when(jnp.logical_not(there))
-            def _():
-                pltpu.make_async_remote_copy(
-                    src_ref=src, dst_ref=dst, send_sem=flux_send.at[step, par], recv_sem=flux_recv.at[step, par],
-                    device_id=at(q, half_a), device_id_type=MESH,
-                ).start()
-
-            @pl.when(there)
-            def _():
-                pltpu.make_async_copy(src, dst, self_sem.at[step, par, 1]).start()
-            return c
-
-        lax.fori_loop(0, na, put, 0)
+        place = lax.rem(a, 2) * no + o
+
+        def put(atm):
+            atm = lax.rem(atm + na, na)
+            return pltpu.make_async_remote_copy(
+                src_ref=flux_tx.at[step, par, atm], dst_ref=flux_rx.at[step, par, place],
+                send_sem=flux_send.at[step, par], recv_sem=flux_recv.at[step, par],
+                device_id=at(atm, half_a), device_id_type=MESH,
+            )
+
+        put(a + na // 2).start()
+
+        def put_pair(n, c):
+            put(a + na // 2 + n).start()
+            put(a + na // 2 - n).start()
+            return c
+
+        lax.fori_loop(1, na // 2, put_pair, 0)
+
+        @pl.when(jnp.logical_not(mine))
+        def _():
+            put(a).start()
+
+        @pl.when(mine)
+        def _():
+            pltpu.make_async_copy(
+                flux_tx.at[step, par, a], flux_rx.at[step, par, place], self_sem.at[step, par, 1]
+            ).start()
 
     def rows_of(buf, sem_send, sem_recv, step, par, count):
         part = buf.at[step, par, pl.ds(0, count)]
@@ -260,20 +266,39 @@
                 copy.wait_send()
 
 
+    sort_sea(0)
+    make_sst(0, 0)
+
     @pl.when(mine)
     def _():
-        pl.semaphore_wait(barrier, 2 * na + 6)
+        pl.semaphore_wait(barrier, na + 7)
 
     @pl.when(jnp.logical_not(mine))
     def _():
-        pl.semaphore_wait(barrier, 2 * na + 8)
+        pl.semaphore_wait(barrier, na + 8)
+
+    send_sst(0, 0)
+    sort_sea(1)
+    make_sst(0, 1)
+    send_sst(0, 1)
+    loads[1].wait()
+    for w in range(4):
+        tok_sky[w] = raw_sky[:, :, :, 128 * w : 128 * w + 128].astype(F32).reshape(8 * na, 128)
+
+    def sort_sky(cc, c):
+        for par in range(2):
+            for w in range(4):
+                part = tok_sky[w, pl.ds(par * 4 * na + cc, na, stride=4), :]
+                air[0, par, cc, :, 128 * w : 128 * w + 128] = part.astype(BF16)
+        return c
+
+    lax.fori_loop(0, 4, sort_sky, 0)
 
     for par in range(2):
         start(put_air(0, par))
-    for par in range(2):
-        send_sst(0, par)
-    for par in range(2):
-        start(put_sea(0, par))
+    start(put_sea(0, 0))
+
+    lax.fori_loop(0, 32, cell_table, 0)
 
     for load in loads[3:]:
         load.wait()
@@ -349,13 +374,19 @@
         flux_tx[step, par] = lines.reshape(na, 1, 128)
         send_flux(step, par)
 
-        @pl.when(step + 1 < NSTEP)
-        def _():
-            start(put_air(step + 1, par))
-
         @pl.when(step + 1 == NSTEP)
         def _():
-            pltpu.make_async_copy(air.at[step + 1, par], sky_out.at[par], out_sem.at[par]).start()
+            def unsort(cc, c):
+                for w in range(4):
+                    part = air[step + 1, par, cc, :, 128 * w : 128 * w + 128].astype(F32)
+                    tok_sky[w, pl.ds(par * 4 * na + cc, na, stride=4), :] = part
+                return c
+
+            lax.fori_loop(0, 4, unsort, 0)
+            rows = pl.ds(pl.multiple_of(par * 4 * na, 4 * na), 4 * na)
+            for w in range(4):
+                raw_sky[par, 0, :, 128 * w : 128 * w + 128] = tok_sky[w, rows, :].astype(BF16)
+            pltpu.make_async_copy(raw_sky.at[par], sky_out.at[par], out_sem.at[par]).start()
 
     def sea_part(step, par):
         for copy in put_sea(step, par):
@@ -383,8 +414,8 @@
 
         @pl.when(step + 1 < NSTEP)
         def _():
+            make_sst(step + 1, par)
             send_sst(step + 1, par)
-            start(put_sea(step + 1, par))
 
         @pl.when(step + 1 == NSTEP)
         def _():
@@ -402,7 +433,19 @@
             return c
 
         lax.fori_loop(0, 2, sky_loop, 0)
+
+        @pl.when(step + 1 < NSTEP)
+        def _():
+            for par in range(2):
+                start(put_air(step + 1, par))
+
+        start(put_sea(step, 1))
         lax.fori_loop(0, 2, sea_loop, 0)
+
+        @pl.when(step + 1 < NSTEP)
+        def _():
+            start(put_sea(step + 1, 0))
+
         return c
 
     lax.fori_loop(0, NSTEP, one_step, 0)
@@ -417,7 +460,7 @@
 
     lax.fori_loop(0, 2 * NSTEP, close, 0)
     for par in range(2):
-        pltpu.make_async_copy(air.at[NSTEP, par], sky_out.at[par], out_sem.at[par]).wait()
+        pltpu.make_async_copy(raw_sky.at[par], sky_out.at[par], out_sem.at[par]).wait()
         pltpu.make_async_copy(
             ocean.at[NSTEP, par, pl.ds(1, 4), pl.ds(1, 8)], sea_out.at[par], out_sem.at[2 + par]
         ).wait()
@@ -435,7 +478,7 @@
     sky_new, sea_new = pl.pallas_call(
         functools.partial(kernel, na, no),
         out_shape=(
-            jax.ShapeDtypeStruct((p, 4, na, 512), BF16),
+            jax.ShapeDtypeStruct(sky.shape, BF16),
             jax.ShapeDtypeStruct((p, 4, 8, no, 256), BF16),
         ),
         in_specs=[smem] * 4 + [hbm] * len(big),
@@ -479,7 +522,6 @@
         ),
         name="coupled_steps",
     )(above, beneath, cover.transpose(0, 2, 1), sea_flag, *big)
-    sky_new = sky_new.transpose(0, 2, 1, 3).reshape(sky.shape)
     sea_new = sea_new.transpose(3, 0, 1, 2, 4).reshape(sea.shape)
     return sky_new, sea_new
 

time: 96.3 us -> 87.2 us (0.906)
  the two profiles are of different devices: /device:TPU:1 before, /device:TPU:8 now
where the time goes in v2:
time: 87.2 us; the launch traced here: 87 us
  Pallas kernels  82.3 us (94%)
  local copies, waits for them, and re-layouts  2.74 us (3%)
  between operations  1.94 us (2%)
    pallas_call x1, Pallas kernels, local(): pl.pallas_call(functools.partial(kernel, na, no), out_shape=(jax.ShapeDty...  82.3 us
    transpose x1, local copies, waits for them, and re-layouts, local(): sea_new = sea_new.transpose(3, 0, 1, 2, 4).reshape(sea.shape)  2.04 us

profile of v2, /device:TPU:8, one launch (start us, length us, event | category | flops | bytes accessed | tf_op | source)
XLA Modules:
  0.0 87.0 jit_solution(15278396482159629255)
XLA Ops:
  1.9 82.3 %coupled_steps.1 = (bf16[2,1,128,512]{3,2,1,0:T(8,128)(2,1)}, bf16[2,4,8,16,256]{4,3,2,1,0:T(8,128)(2,1)}) custom-call(s32[1]{0:T(128)S(6)} %copy.22.above, s32[1]{0:T(128)S(6)} %copy.23.beneath, s32[4,4,8]{2,1,0:T(4,128)} %bitcast.10, s32[4,8]{1,0:T(4,128)} %sea_flag.1, bf16[2,1,128,512]{3,2,1,0:T(8,128)(2,1)} %sky.1, bf16[32,4,8,256]{3,2,1,0:T(8,128)(2,1)} %sea.1, ...), custom_call_target="tpu_custom_call" | custom-call | tf_op jit(solution)/shard_map/coupled_steps/pallas_call | solution.py:478
  84.2 0.0 copy-start
  84.2 2.0 %copy.20 = bf16[16,2,4,8,256]{4,3,2,1,0:T(8,128)(2,1)} copy(bf16[16,2,4,8,256]{4,0,3,2,1:T(8,128)(2,1)} %bitcast.8) | data formatting | bytes 1048576 | tf_op jit(solution)/shard_map/transpose | solution.py:525
  86.2 0.0 copy-done
  86.3 0.7 copy.24
Async XLA Ops:
  84.2 2.0 %copy-start = (bf16[2,1,128,512]{3,2,1,0:T(8,128)(2,1)S(1)}, bf16[2,1,128,512]{3,2,1,0:T(8,128)(2,1)}, u32[]{:S(2)}) copy-start(bf16[2,1,128,512]{3,2,1,0:T(8,128)(2,1)} %get-tuple-element.8) | copy-start | bytes 786436

commit v3 on v2

--- a/solution.py
+++ b/solution.py
@@ -11,13 +11,12 @@
 F32 = jnp.float32
 BF16 = jnp.bfloat16
 NSTEP = 2
-SIDES = [(-1, 0), (1, 0), (0, -1), (0, 1), (-1, -1), (-1, 1), (1, -1), (1, 1)]
-
-
-def gelu(x):
+SIDES = [(-1, 0), (1, 0), (0, -1), (0, 1)]
+
+
+def gelu_twice(x):
     inner = x * (0.7978845608028654 + 0.035677408136300125 * (x * x))
-    half = 0.5 * x
-    return half + half * jnp.tanh(inner)
+    return x * (1.0 + jnp.tanh(inner))
 
 
 def normed(z, gain):
@@ -39,7 +38,7 @@
     sky_out, sea_out,
     raw_sky, raw_sea, v_sky_filter, v_sky_gain, v_heat, v_sky_in, v_sky_back, v_to_flux, v_sea_filter, v_sea_gain, v_from_flux,
     v_sea_in, v_sea_back, v_to_sst,
-    tok_sky, tok_sea, air, up, down, ocean, ext, zbuf, ubuf, hbuf,
+    tok_sky, tok_sea, air, up, down, ocean, share_tx, share_rx, ext, zbuf, ubuf, hbuf, zsea, usea, hsea,
     flux_wide, heat_wide, into_wide, sst_wide, cellw, seaw, poolw,
     sst_tx, sst_rx, flux_tx, flux_rx,
     in_sem, sst_send, sst_recv, flux_send, flux_recv, self_sem, air_send, air_recv, sea_send, sea_recv, out_sem,
@@ -90,7 +89,7 @@
         r0, c0 = row // 2 * 2, col // 2 * 2
         count = sea_flag[r0, c0] + sea_flag[r0, c0 + 1] + sea_flag[r0 + 1, c0] + sea_flag[r0 + 1, c0 + 1]
         count = jnp.full((no, 256), count, jnp.int32).astype(F32)
-        seaw[cell] = flag
+        seaw[cell] = 0.5 * flag
         poolw[cell] = flag / jnp.maximum(count, 1.0)
         return c
 
@@ -140,21 +139,38 @@
             for n, (there, da) in enumerate([(up, 1), (down, -1)])
         ]
 
-    def put_sea(step, par):
-        copies = []
-        for n, (di, dj) in enumerate(SIDES):
-            rows = {-1: 1, 0: pl.ds(1, 4), 1: 4}[di]
-            cols = {-1: 1, 0: pl.ds(1, 8), 1: 8}[dj]
-            to_rows = {-1: 5, 0: pl.ds(1, 4), 1: 0}[di]
-            to_cols = {-1: 9, 0: pl.ds(1, 8), 1: 0}[dj]
-            copies.append(
-                pltpu.make_async_remote_copy(
-                    src_ref=ocean.at[step, par, rows, cols], dst_ref=ocean.at[step, par, to_rows, to_cols],
-                    send_sem=sea_send.at[step, par, n], recv_sem=sea_recv.at[step, par, n],
-                    device_id=at(a + dj, o + di), device_id_type=MESH,
-                )
+    def put_cols(step, par):
+        return [
+            pltpu.make_async_remote_copy(
+                src_ref=ocean.at[step, par, pl.ds(1, 4), src], dst_ref=ocean.at[step, par, pl.ds(1, 4), dst],
+                send_sem=sea_send.at[step, par, n], recv_sem=sea_recv.at[step, par, n],
+                device_id=at(a + da, o), device_id_type=MESH,
             )
-        return copies
+            for n, (src, dst, da) in enumerate([(8, 0, 1), (1, 9, -1)])
+        ]
+
+    def put_rows(step, par):
+        return [
+            pltpu.make_async_remote_copy(
+                src_ref=share_tx.at[step, par, n], dst_ref=share_rx.at[step, par, n],
+                send_sem=sea_send.at[step, par, 2 + n], recv_sem=sea_recv.at[step, par, 2 + n],
+                device_id=at(a, o + do), device_id_type=MESH,
+            )
+            for n, do in enumerate([1, -1])
+        ]
+
+    def send_rows(step, par):
+        for copy in put_cols(step, par):
+            copy.wait_recv()
+        for n, (row, i) in enumerate([(4, 0), (1, 2)]):
+            for w in range(2):
+                part = slice(128 * w, 128 * w + 128)
+                cells = ocean[step, par, row, :, :, part].astype(F32)
+                z = jnp.zeros((8, no, 128), F32)
+                for j in range(3):
+                    z = z + v_sea_filter[3 * i + j : 3 * i + j + 1, part][None] * cells[j : j + 8]
+                share_tx[step, par, n, :, :, part] = z.astype(BF16)
+        start(put_rows(step, par))
 
     def start(copies):
         for copy in copies:
@@ -178,7 +194,8 @@
             sst_tx[step, par, pl.ds(rr * no, no)] = lines.reshape(no, 1, 128)
             return c
 
-        lax.fori_loop(0, 2, block_rows, 0)
+        for rr in range(2):
+            block_rows(rr, 0)
 
     def send_sst(step, par):
         def put(ocn, rr):
@@ -271,11 +288,11 @@
 
     @pl.when(mine)
     def _():
-        pl.semaphore_wait(barrier, na + 7)
+        pl.semaphore_wait(barrier, na + 3)
 
     @pl.when(jnp.logical_not(mine))
     def _():
-        pl.semaphore_wait(barrier, na + 8)
+        pl.semaphore_wait(barrier, na + 4)
 
     send_sst(0, 0)
     sort_sea(1)
@@ -295,8 +312,8 @@
     lax.fori_loop(0, 4, sort_sky, 0)
 
     for par in range(2):
+        start(put_cols(0, par))
         start(put_air(0, par))
-    start(put_sea(0, 0))
 
     lax.fori_loop(0, 32, cell_table, 0)
 
@@ -312,6 +329,8 @@
         spread_over_lanes(16, 128), v_from_flux[...].astype(BF16), (((0,), (0,)), ((), ())), preferred_element_type=F32
     ).astype(BF16)
 
+    send_rows(0, 0)
+
     turns = []
     for code in (above[0], beneath[0]):
         cosine = jnp.where(code == 0, 1.0, 0.0) - jnp.where(code == 2, 1.0, 0.0)
@@ -350,21 +369,23 @@
             zbuf[cc] = jnp.dot(one, heat_wide[...], preferred_element_type=F32)
 
         def column(cc, c):
-            z = zbuf[cc]
-            for i in range(3):
-                for j in range(3):
-                    z = z + v_sky_filter[3 * i + j : 3 * i + j + 1, :] * ext[i, cc + j]
-            ubuf[cc] = normed(z, v_sky_gain[...])
+            for w in range(2):
+                part = slice(256 * w, 256 * w + 256)
+                z = zbuf[cc, :, part]
+                for i in range(3):
+                    for j in range(3):
+                        z = z + v_sky_filter[3 * i + j : 3 * i + j + 1, part] * ext[i, cc + j, :, part]
+                zbuf[cc, :, part] = z
             return c
 
         lax.fori_loop(0, 4, column, 0)
-        u = ubuf[...].reshape(4 * na, 512)
+        ubuf[...] = normed(zbuf[...].reshape(4 * na, 512), v_sky_gain[...])
         for n in range(4):
             part = slice(256 * n, 256 * n + 256)
-            hbuf[:, part] = gelu(jnp.dot(u, v_sky_in[:, part], preferred_element_type=F32)).astype(BF16)
+            hbuf[:, part] = gelu_twice(jnp.dot(ubuf[...], v_sky_in[:, part], preferred_element_type=F32)).astype(BF16)
         for n in range(2):
             part = slice(256 * n, 256 * n + 256)
-            change = jnp.dot(hbuf[...], v_sky_back[:, part], preferred_element_type=F32)
+            change = 0.5 * jnp.dot(hbuf[...], v_sky_back[:, part], preferred_element_type=F32)
             old = air[step, par, :, :, part].astype(F32)
             air[step + 1, par, :, :, part] = (old + change.reshape(4, na, 256)).astype(BF16)
         lines = jnp.zeros((na, 128), F32)
@@ -389,33 +410,50 @@
             pltpu.make_async_copy(raw_sky.at[par], sky_out.at[par], out_sem.at[par]).start()
 
     def sea_part(step, par):
-        for copy in put_sea(step, par):
-            copy.wait_recv()
         exchange_wait(flux_rx, flux_send, flux_recv, step, par, 1, True)
         got = flux_rx[step, par].reshape(2 * no, 128)
         fields = jnp.where(lane < 64, got[:no], got[no:])
 
-        def line(row, c):
-            cells = pl.ds(pl.multiple_of(row * 8, 8), 8)
-            lhs = (cellw[cells] * fields[None]).astype(BF16).reshape(8 * no, 128)
-            z = jnp.dot(lhs, into_wide[...], preferred_element_type=F32).reshape(8, no, 256)
-            for i in range(3):
-                for j in range(3):
-                    tap = v_sea_filter[3 * i + j : 3 * i + j + 1, :]
-                    z = z + tap[None] * ocean[step, par, row + i, j : j + 8].astype(F32)
-            u = normed(z.reshape(8 * no, 256), v_sea_gain[...])
-            hidden = gelu(jnp.dot(u, v_sea_in[...], preferred_element_type=F32)).astype(BF16)
-            change = jnp.dot(hidden, v_sea_back[...], preferred_element_type=F32).reshape(8, no, 256)
-            old = ocean[step, par, row + 1, 1:9].astype(F32)
-            ocean[step + 1, par, row + 1, 1:9] = (old + seaw[cells] * change).astype(BF16)
-            return c
-
-        lax.fori_loop(0, 4, line, 0)
+        lhs = (cellw[...] * fields[None]).astype(BF16).reshape(32 * no, 128)
+        zsea[...] = jnp.dot(lhs, into_wide[...], preferred_element_type=F32).reshape(4, 8 * no, 256)
+
+        def line(row, c, taps=(0, 1, 2), side=None):
+            for w in range(2):
+                part = slice(128 * w, 128 * w + 128)
+                z = zsea[row, :, part].reshape(8, no, 128)
+                if side is not None:
+                    z = z + share_rx[step, par, side, :, :, part].astype(F32)
+                for i in taps:
+                    cells = ocean[step, par, row + i, :, :, part].astype(F32)
+                    for j in range(3):
+                        z = z + v_sea_filter[3 * i + j : 3 * i + j + 1, part][None] * cells[j : j + 8]
+                zsea[row, :, part] = z.reshape(8 * no, 128)
+            return c
+
+        lax.fori_loop(1, 3, line, 0)
+        for copy in put_rows(step, par):
+            copy.wait_recv()
+        line(0, 0, (1, 2), 0)
+        line(3, 0, (0, 1), 1)
+        rows = 16 * no
+        for m in range(2):
+            usea[rows * m : rows * m + rows] = normed(zsea[2 * m : 2 * m + 2].reshape(rows, 256), v_sea_gain[...])
+        for m in range(2):
+            for n in range(2):
+                part = slice(256 * n, 256 * n + 256)
+                got = jnp.dot(usea[rows * m : rows * m + rows], v_sea_in[:, part], preferred_element_type=F32)
+                hsea[rows * m : rows * m + rows, part] = gelu_twice(got).astype(BF16)
+        for m in range(2):
+            change = jnp.dot(hsea[rows * m : rows * m + rows], v_sea_back[...], preferred_element_type=F32)
+            change = change.reshape(2, 8, no, 256) * seaw[16 * m : 16 * m + 16].reshape(2, 8, no, 256)
+            old = ocean[step, par, 1 + 2 * m : 3 + 2 * m, 1:9].astype(F32)
+            ocean[step + 1, par, 1 + 2 * m : 3 + 2 * m, 1:9] = (old + change).astype(BF16)
 
         @pl.when(step + 1 < NSTEP)
         def _():
             make_sst(step + 1, par)
             send_sst(step + 1, par)
+            start(put_cols(step + 1, par))
 
         @pl.when(step + 1 == NSTEP)
         def _():
@@ -439,12 +477,12 @@
             for par in range(2):
                 start(put_air(step + 1, par))
 
-        start(put_sea(step, 1))
+        send_rows(step, 1)
         lax.fori_loop(0, 2, sea_loop, 0)
 
         @pl.when(step + 1 < NSTEP)
         def _():
-            start(put_sea(step + 1, 0))
+            send_rows(step + 1, 0)
 
         return c
 
@@ -452,7 +490,7 @@
 
     def close(n, c):
         step, par = n // 2, lax.rem(n, 2)
-        for copy in put_air(step, par) + put_sea(step, par):
+        for copy in put_air(step, par) + put_cols(step, par) + put_rows(step, par):
             copy.wait_send()
         exchange_wait(sst_tx, sst_send, sst_recv, step, par, 0, False)
         exchange_wait(flux_tx, flux_send, flux_recv, step, par, 1, False)
@@ -490,10 +528,15 @@
             vmem((n, p, 4, na, 512), BF16),
             vmem((n, p, 4, na, 512), BF16),
             vmem((n + 1, p, 6, 10, no, 256), BF16),
+            vmem((n, p, 2, 8, no, 256), BF16),
+            vmem((n, p, 2, 8, no, 256), BF16),
             vmem((3, 6, na, 512), F32),
             vmem((4, na, 512), F32),
-            vmem((4, na, 512), BF16),
+            vmem((4 * na, 512), BF16),
             vmem((4 * na, 1024), BF16),
+            vmem((4, 8 * no, 256), F32),
+            vmem((32 * no, 256), BF16),
+            vmem((32 * no, 512), BF16),
             vmem((512, 128), BF16),
             vmem((128, 512), BF16),
             vmem((128, 256), BF16),
@@ -513,8 +556,8 @@
             dma((n, p, 2)),
             dma((n, p, 2)),
             dma((n, p, 2)),
-            dma((n, p, 8)),
-            dma((n, p, 8)),
+            dma((n, p, 4)),
+            dma((n, p, 4)),
             dma((4,)),
         ],
         compiler_params=pltpu.CompilerParams(

time: 87.2 us -> 76.3 us (0.87)
  the two profiles are of different devices: /device:TPU:8 before, /device:TPU:1 now
where the time goes in v3:
time: 76.3 us; the launch traced here: 76.1 us
  Pallas kernels  71.4 us (94%)
  local copies, waits for them, and re-layouts  2.74 us (4%)
  between operations  1.94 us (3%)
    pallas_call x1, Pallas kernels, local(): pl.pallas_call(functools.partial(kernel, na, no), out_shape=(jax.ShapeDty...  71.4 us
    transpose x1, local copies, waits for them, and re-layouts, local(): sea_new = sea_new.transpose(3, 0, 1, 2, 4).reshape(sea.shape)  2.04 us

profile of v3, /device:TPU:1, one launch (start us, length us, event | category | flops | bytes accessed | tf_op | source)
XLA Modules:
  0.0 76.1 jit_solution(5181773445204318226)
XLA Ops:
  1.9 71.4 %coupled_steps.1 = (bf16[2,1,128,512]{3,2,1,0:T(8,128)(2,1)}, bf16[2,4,8,16,256]{4,3,2,1,0:T(8,128)(2,1)}) custom-call(s32[1]{0:T(128)S(6)} %copy.22.above, s32[1]{0:T(128)S(6)} %copy.23.beneath, s32[4,4,8]{2,1,0:T(4,128)} %bitcast.10, s32[4,8]{1,0:T(4,128)} %sea_flag.1, bf16[2,1,128,512]{3,2,1,0:T(8,128)(2,1)} %sky.1, bf16[32,4,8,256]{3,2,1,0:T(8,128)(2,1)} %sea.1, ...), custom_call_target="tpu_custom_call" | custom-call | tf_op jit(solution)/shard_map/coupled_steps/pallas_call | solution.py:516
  73.3 0.0 copy-start
  73.3 2.0 %copy.20 = bf16[16,2,4,8,256]{4,3,2,1,0:T(8,128)(2,1)} copy(bf16[16,2,4,8,256]{4,0,3,2,1:T(8,128)(2,1)} %bitcast.8) | data formatting | bytes 1048576 | tf_op jit(solution)/shard_map/transpose | solution.py:568
  75.4 0.0 copy-done
  75.4 0.7 copy.24
Async XLA Ops:
  73.3 2.0 %copy-start = (bf16[2,1,128,512]{3,2,1,0:T(8,128)(2,1)S(1)}, bf16[2,1,128,512]{3,2,1,0:T(8,128)(2,1)}, u32[]{:S(2)}) copy-start(bf16[2,1,128,512]{3,2,1,0:T(8,128)(2,1)} %get-tuple-element.8) | copy-start | bytes 786436

commit v4 on v3

--- a/solution.py
+++ b/solution.py
@@ -33,9 +33,10 @@
 
 def kernel(
     na, no,
-    above, beneath, cover, sea_flag,
+    above_in, beneath_in, cover_in, flag_in,
     sky, sea, sky_filter, sky_gain, heat, sky_in, sky_back, to_flux, sea_filter, sea_gain, from_flux, sea_in, sea_back, to_sst,
     sky_out, sea_out,
+    above, beneath, cover, sea_flag,
     raw_sky, raw_sea, v_sky_filter, v_sky_gain, v_heat, v_sky_in, v_sky_back, v_to_flux, v_sea_filter, v_sea_gain, v_from_flux,
     v_sea_in, v_sea_back, v_to_sst,
     tok_sky, tok_sea, air, up, down, ocean, share_tx, share_rx, ext, zbuf, ubuf, hbuf, zsea, usea, hsea,
@@ -57,14 +58,16 @@
     loads = [
         pltpu.make_async_copy(src, dst, in_sem.at[n])
         for n, (src, dst) in enumerate([
-            (sea, raw_sea), (sky, raw_sky), (to_sst, v_to_sst), (sky_filter, v_sky_filter), (heat, v_heat),
+            (sea.at[:, 0], raw_sea.at[0]), (sky, raw_sky), (to_sst, v_to_sst), (sky_filter, v_sky_filter), (heat, v_heat),
             (sky_gain, v_sky_gain), (sky_in, v_sky_in), (sky_back, v_sky_back), (to_flux, v_to_flux),
             (sea_filter, v_sea_filter), (sea_gain, v_sea_gain), (from_flux, v_from_flux), (sea_in, v_sea_in),
-            (sea_back, v_sea_back),
+            (sea_back, v_sea_back), (flag_in, sea_flag), (cover_in, cover), (above_in, above), (beneath_in, beneath),
+            (sea.at[:, 1], raw_sea.at[1]),
         ])
     ]
-    for load in loads:
-        load.start()
+    loads[0].start()
+    loads[14].start()
+    loads[18].start()
 
     barrier = pltpu.get_barrier_semaphore()
 
@@ -80,6 +83,9 @@
 
     for di, dj in SIDES:
         pl.semaphore_signal(barrier, inc=1, device_id=at(a + dj, o + di), device_id_type=MESH)
+
+    for load in loads[1:14] + loads[15:18]:
+        load.start()
 
     lane = lax.broadcasted_iota(jnp.int32, (no, 128), 1)
 
@@ -93,6 +99,7 @@
         poolw[cell] = flag / jnp.maximum(count, 1.0)
         return c
 
+    loads[14].wait()
     lax.fori_loop(0, 32, pool_table, 0)
 
     def cell_table(cell, c):
@@ -103,23 +110,19 @@
         cellw[cell] = share
         return c
 
-    loads[0].wait()
-    per = 2 * no // 4
-
-    def open_sea(n, c):
-        part = raw_sea[pl.ds(n * per, per)].astype(F32)
-        part = part.reshape(per * 32, 256)
+    def open_sea(par):
+        loads[18 * par].wait()
         for w in range(2):
-            tok_sea[w, pl.ds(pl.multiple_of(n * per * 32, per * 32), per * 32), :] = part[:, 128 * w : 128 * w + 128]
-        return c
-
-    lax.fori_loop(0, 4, open_sea, 0)
+            part = raw_sea[par, :, :, :, 128 * w : 128 * w + 128].astype(F32)
+            tok_sea[par, w] = part.reshape(32 * no, 128)
 
     def sort_sea(par):
+        open_sea(par)
+
         def sort_cell(cell, c):
             row, col = cell // 8, lax.rem(cell, 8)
             for w in range(2):
-                part = tok_sea[w, pl.ds(par * 32 + cell, no, stride=64), :]
+                part = tok_sea[par, w, pl.ds(cell, no, stride=32), :]
                 ocean[0, par, 1 + row, 1 + col, :, 128 * w : 128 * w + 128] = part.astype(BF16)
             return c
 
@@ -315,9 +318,10 @@
         start(put_cols(0, par))
         start(put_air(0, par))
 
+    loads[15].wait()
     lax.fori_loop(0, 32, cell_table, 0)
 
-    for load in loads[3:]:
+    for load in loads[3:14] + loads[16:18]:
         load.wait()
     flux_wide[...] = lax.dot_general(
         v_to_flux[...], spread_over_lanes(16, 128), (((0,), (0,)), ((), ())), preferred_element_type=F32
@@ -339,7 +343,7 @@
 
     lane_a = lax.broadcasted_iota(jnp.int32, (na, 128), 1)
 
-    def sky_part(step, par):
+    def sky_stencil(step, par):
         for copy in put_air(step, par):
             copy.wait_recv()
 
@@ -362,24 +366,24 @@
 
         lax.fori_loop(0, 3, ends, 0)
 
-        exchange_wait(sst_rx, sst_send, sst_recv, step, par, 0, True)
-        fields = sst_rx[step, par].reshape(na, 128)
-        for cc in range(4):
-            one = jnp.where(lane_a // 8 == cc, fields, 0.0).astype(BF16)
-            zbuf[cc] = jnp.dot(one, heat_wide[...], preferred_element_type=F32)
-
         def column(cc, c):
             for w in range(2):
                 part = slice(256 * w, 256 * w + 256)
-                z = zbuf[cc, :, part]
+                z = jnp.zeros((na, 256), F32)
                 for i in range(3):
                     for j in range(3):
                         z = z + v_sky_filter[3 * i + j : 3 * i + j + 1, part] * ext[i, cc + j, :, part]
-                zbuf[cc, :, part] = z
+                zbuf[par, cc, :, part] = z
             return c
 
         lax.fori_loop(0, 4, column, 0)
-        ubuf[...] = normed(zbuf[...].reshape(4 * na, 512), v_sky_gain[...])
+
+    def sky_part(step, par):
+        exchange_wait(sst_rx, sst_send, sst_recv, step, par, 0, True)
+        fields = sst_rx[step, par].reshape(na, 128)
+        lhs = [jnp.where(lane_a // 8 == cc, fields, 0.0).astype(BF16) for cc in range(4)]
+        warm = jnp.dot(jnp.concatenate(lhs, axis=0), heat_wide[...], preferred_element_type=F32)
+        ubuf[...] = normed(warm + zbuf[par].reshape(4 * na, 512), v_sky_gain[...])
         for n in range(4):
             part = slice(256 * n, 256 * n + 256)
             hbuf[:, part] = gelu_twice(jnp.dot(ubuf[...], v_sky_in[:, part], preferred_element_type=F32)).astype(BF16)
@@ -409,35 +413,39 @@
                 raw_sky[par, 0, :, 128 * w : 128 * w + 128] = tok_sky[w, rows, :].astype(BF16)
             pltpu.make_async_copy(raw_sky.at[par], sky_out.at[par], out_sem.at[par]).start()
 
+    def sea_line(step, par, row, taps, side):
+        for w in range(2):
+            part = slice(128 * w, 128 * w + 128)
+            z = jnp.zeros((8, no, 128), F32) if side is None else share_rx[step, par, side, :, :, part].astype(F32)
+            for i in taps:
+                cells = ocean[step, par, row + i, :, :, part].astype(F32)
+                for j in range(3):
+                    z = z + v_sea_filter[3 * i + j : 3 * i + j + 1, part][None] * cells[j : j + 8]
+            zsea[par, row, :, part] = z.reshape(8 * no, 128)
+
+    def sea_middle(step, par):
+        def line(row, c):
+            sea_line(step, par, row, (0, 1, 2), None)
+            return c
+
+        lax.fori_loop(1, 3, line, 0)
+
+    def sea_edges(step, par):
+        for copy in put_rows(step, par):
+            copy.wait_recv()
+        sea_line(step, par, 0, (1, 2), 0)
+        sea_line(step, par, 3, (0, 1), 1)
+
     def sea_part(step, par):
         exchange_wait(flux_rx, flux_send, flux_recv, step, par, 1, True)
         got = flux_rx[step, par].reshape(2 * no, 128)
         fields = jnp.where(lane < 64, got[:no], got[no:])
-
-        lhs = (cellw[...] * fields[None]).astype(BF16).reshape(32 * no, 128)
-        zsea[...] = jnp.dot(lhs, into_wide[...], preferred_element_type=F32).reshape(4, 8 * no, 256)
-
-        def line(row, c, taps=(0, 1, 2), side=None):
-            for w in range(2):
-                part = slice(128 * w, 128 * w + 128)
-                z = zsea[row, :, part].reshape(8, no, 128)
-                if side is not None:
-                    z = z + share_rx[step, par, side, :, :, part].astype(F32)
-                for i in taps:
-                    cells = ocean[step, par, row + i, :, :, part].astype(F32)
-                    for j in range(3):
-                        z = z + v_sea_filter[3 * i + j : 3 * i + j + 1, part][None] * cells[j : j + 8]
-                zsea[row, :, part] = z.reshape(8 * no, 128)
-            return c
-
-        lax.fori_loop(1, 3, line, 0)
-        for copy in put_rows(step, par):
-            copy.wait_recv()
-        line(0, 0, (1, 2), 0)
-        line(3, 0, (0, 1), 1)
         rows = 16 * no
         for m in range(2):
-            usea[rows * m : rows * m + rows] = normed(zsea[2 * m : 2 * m + 2].reshape(rows, 256), v_sea_gain[...])
+            lhs = (cellw[16 * m : 16 * m + 16] * fields[None]).astype(BF16).reshape(rows, 128)
+            forced = jnp.dot(lhs, into_wide[...], preferred_element_type=F32)
+            z = forced + zsea[par, 2 * m : 2 * m + 2].reshape(rows, 256)
+            usea[rows * m : rows * m + rows] = normed(z, v_sea_gain[...])
         for m in range(2):
             for n in range(2):
                 part = slice(256 * n, 256 * n + 256)
@@ -461,16 +469,17 @@
                 ocean.at[step + 1, par, pl.ds(1, 4), pl.ds(1, 8)], sea_out.at[par], out_sem.at[2 + par]
             ).start()
 
+    def both(step, *parts):
+        def run(par, c):
+            for part in parts:
+                part(step, par)
+            return c
+
+        lax.fori_loop(0, 2, run, 0)
+
     def one_step(step, c):
-        def sky_loop(par, c):
-            sky_part(step, par)
-            return c
-
-        def sea_loop(par, c):
-            sea_part(step, par)
-            return c
-
-        lax.fori_loop(0, 2, sky_loop, 0)
+        both(step, sky_stencil)
+        both(step, sky_part)
 
         @pl.when(step + 1 < NSTEP)
         def _():
@@ -478,7 +487,8 @@
                 start(put_air(step + 1, par))
 
         send_rows(step, 1)
-        lax.fori_loop(0, 2, sea_loop, 0)
+        both(step, sea_middle)
+        both(step, sea_edges, sea_part)
 
         @pl.when(step + 1 < NSTEP)
         def _():
@@ -506,24 +516,26 @@
 
 def local(na, no, sky, sea, above, beneath, cover, sea_flag, sky_filter, sky_gain, heat, sky_in, sky_back, to_flux,
           sea_filter, sea_gain, from_flux, sea_in, sea_back, to_sst):
-    smem = pl.BlockSpec(memory_space=pltpu.SMEM)
     hbm = pl.BlockSpec(memory_space=pl.ANY)
     vmem = pltpu.VMEM
     dma = pltpu.SemaphoreType.DMA
     n, p = NSTEP, 2
-    big = [sky, sea, sky_filter, sky_gain[None], heat, sky_in, sky_back, to_flux.T, sea_filter, sea_gain[None], from_flux, sea_in,
+    big = [sky, sea.reshape(no, 2, *sea.shape[1:]), sky_filter, sky_gain[None], heat, sky_in, sky_back, to_flux.T, sea_filter, sea_gain[None], from_flux, sea_in,
            sea_back, to_sst.T]
+    small = [above, beneath, cover.transpose(0, 2, 1), sea_flag]
     sky_new, sea_new = pl.pallas_call(
         functools.partial(kernel, na, no),
         out_shape=(
             jax.ShapeDtypeStruct(sky.shape, BF16),
             jax.ShapeDtypeStruct((p, 4, 8, no, 256), BF16),
         ),
-        in_specs=[smem] * 4 + [hbm] * len(big),
+        in_specs=[hbm] * (4 + len(big)),
         out_specs=(hbm, hbm),
-        scratch_shapes=[vmem(x.shape, x.dtype) for x in big] + [
+        scratch_shapes=[pltpu.SMEM(x.shape, x.dtype) for x in small] + [vmem(x.shape, x.dtype) for x in big[:1]] + [
+            vmem((2, no, *sea.shape[1:]), BF16)
+        ] + [vmem(x.shape, x.dtype) for x in big[2:]] + [
             vmem((4, p * 4 * na, 128), F32),
-            vmem((2, 2 * no * 32, 128), F32),
+            vmem((2, 2, no * 32, 128), F32),
             vmem((n + 1, p, 4, na, 512), BF16),
             vmem((n, p, 4, na, 512), BF16),
             vmem((n, p, 4, na, 512), BF16),
@@ -531,10 +543,10 @@
             vmem((n, p, 2, 8, no, 256), BF16),
             vmem((n, p, 2, 8, no, 256), BF16),
             vmem((3, 6, na, 512), F32),
-            vmem((4, na, 512), F32),
+            vmem((p, 4, na, 512), F32),
             vmem((4 * na, 512), BF16),
             vmem((4 * na, 1024), BF16),
-            vmem((4, 8 * no, 256), F32),
+            vmem((p, 4, 8 * no, 256), F32),
             vmem((32 * no, 256), BF16),
             vmem((32 * no, 512), BF16),
             vmem((512, 128), BF16),
@@ -548,7 +560,7 @@
             vmem((n, p, na, 1, 128), F32),
             vmem((n, p, na, 1, 128), F32),
             vmem((n, p, na, 1, 128), F32),
-            dma((len(big),)),
+            dma((len(small) + len(big) + 1,)),
             dma((n, p)),
             dma((n, p)),
             dma((n, p)),
@@ -564,7 +576,7 @@
             collective_id=0, has_side_effects=True, vmem_limit_bytes=56 * 1024 * 1024
         ),
         name="coupled_steps",
-    )(above, beneath, cover.transpose(0, 2, 1), sea_flag, *big)
+    )(*small, *big)
     sea_new = sea_new.transpose(3, 0, 1, 2, 4).reshape(sea.shape)
     return sky_new, sea_new
 

time: 76.3 us -> 75.7 us (level)
  Pallas kernels: 71.4 us -> 70.5 us
    pallas_call x1, Pallas kernels: 71.4 us -> 70.5 us  [local(): pl.pallas_call(functools.partial(kernel, na, no), out_shape=(jax.ShapeDty...]
where the time goes in v4:
time: 75.7 us; the launch traced here: 75.2 us
  Pallas kernels  70.5 us (93%)
  local copies, waits for them, and re-layouts  2.74 us (4%)
  between operations  1.94 us (3%)
    pallas_call x1, Pallas kernels, local(): pl.pallas_call(functools.partial(kernel, na, no), out_shape=(jax.ShapeDty...  70.5 us
    transpose x1, local copies, waits for them, and re-layouts, local(): sea_new = sea_new.transpose(3, 0, 1, 2, 4).reshape(sea.shape)  2.04 us

profile of v4, /device:TPU:1, one launch (start us, length us, event | category | flops | bytes accessed | tf_op | source)
XLA Modules:
  0.0 75.2 jit_solution(2215604620279267158)
XLA Ops:
  1.9 70.5 %coupled_steps.1 = (bf16[2,1,128,512]{3,2,1,0:T(8,128)(2,1)}, bf16[2,4,8,16,256]{4,3,2,1,0:T(8,128)(2,1)}) custom-call(s32[1]{0:T(128)S(6)} %copy.22.above_in, s32[1]{0:T(128)S(6)} %copy.23.beneath_in, s32[4,4,8]{2,1,0:T(4,128)} %bitcast.12, s32[4,8]{1,0:T(4,128)} %flag_in.1, bf16[2,1,128,512]{3,2,1,0:T(8,128)(2,1)} %sky.1, ...), custom_call_target="tpu_custom_call" | custom-call | tf_op jit(solution)/shard_map/coupled_steps/pallas_call | solution.py:526
  72.5 0.0 copy-start
  72.5 2.0 %copy.20 = bf16[16,2,4,8,256]{4,3,2,1,0:T(8,128)(2,1)} copy(bf16[16,2,4,8,256]{4,0,3,2,1:T(8,128)(2,1)} %bitcast.9) | data formatting | bytes 1048576 | tf_op jit(solution)/shard_map/transpose | solution.py:580
  74.5 0.0 copy-done
  74.5 0.7 copy.24
Async XLA Ops:
  72.5 2.0 %copy-start = (bf16[2,1,128,512]{3,2,1,0:T(8,128)(2,1)S(1)}, bf16[2,1,128,512]{3,2,1,0:T(8,128)(2,1)}, u32[]{:S(2)}) copy-start(bf16[2,1,128,512]{3,2,1,0:T(8,128)(2,1)} %get-tuple-element.8) | copy-start | bytes 786436

commit v5 on v4

--- a/solution.py
+++ b/solution.py
@@ -481,12 +481,13 @@
         both(step, sky_stencil)
         both(step, sky_part)
 
+        send_rows(step, 1)
+
         @pl.when(step + 1 < NSTEP)
         def _():
             for par in range(2):
                 start(put_air(step + 1, par))
 
-        send_rows(step, 1)
         both(step, sea_middle)
         both(step, sea_edges, sea_part)
 

time: 75.7 us -> 74.9 us (0.989)
  Pallas kernels: 70.5 us -> 69.6 us
    pallas_call x1, Pallas kernels: 70.5 us -> 69.6 us  [local(): pl.pallas_call(functools.partial(kernel, na, no), out_shape=(jax.ShapeDty...]
where the time goes in v5:
time: 74.9 us; the launch traced here: 74.3 us
  Pallas kernels  69.6 us (93%)
  local copies, waits for them, and re-layouts  2.74 us (4%)
  between operations  1.94 us (3%)
    pallas_call x1, Pallas kernels, local(): pl.pallas_call(functools.partial(kernel, na, no), out_shape=(jax.ShapeDty...  69.6 us
    transpose x1, local copies, waits for them, and re-layouts, local(): sea_new = sea_new.transpose(3, 0, 1, 2, 4).reshape(sea.shape)  2.04 us

profile of v5, /device:TPU:1, one launch (start us, length us, event | category | flops | bytes accessed | tf_op | source)
XLA Modules:
  0.0 74.3 jit_solution(10458152817862300271)
XLA Ops:
  1.9 69.6 %coupled_steps.1 = (bf16[2,1,128,512]{3,2,1,0:T(8,128)(2,1)}, bf16[2,4,8,16,256]{4,3,2,1,0:T(8,128)(2,1)}) custom-call(s32[1]{0:T(128)S(6)} %copy.22.above_in, s32[1]{0:T(128)S(6)} %copy.23.beneath_in, s32[4,4,8]{2,1,0:T(4,128)} %bitcast.12, s32[4,8]{1,0:T(4,128)} %flag_in.1, bf16[2,1,128,512]{3,2,1,0:T(8,128)(2,1)} %sky.1, ...), custom_call_target="tpu_custom_call" | custom-call | tf_op jit(solution)/shard_map/coupled_steps/pallas_call | solution.py:527
  71.6 0.0 copy-start
  71.6 2.0 %copy.20 = bf16[16,2,4,8,256]{4,3,2,1,0:T(8,128)(2,1)} copy(bf16[16,2,4,8,256]{4,0,3,2,1:T(8,128)(2,1)} %bitcast.9) | data formatting | bytes 1048576 | tf_op jit(solution)/shard_map/transpose | solution.py:581
  73.6 0.0 copy-done
  73.6 0.7 copy.24
Async XLA Ops:
  71.6 2.0 %copy-start = (bf16[2,1,128,512]{3,2,1,0:T(8,128)(2,1)S(1)}, bf16[2,1,128,512]{3,2,1,0:T(8,128)(2,1)}, u32[]{:S(2)}) copy-start(bf16[2,1,128,512]{3,2,1,0:T(8,128)(2,1)} %get-tuple-element.8) | copy-start | bytes 786436
